TPU v7x, 32 devices: a whole 2x2x4 slice. The times are simulated.
32 devices in a mesh: section: 2 (over x), seq: 4 (over y, core), tensor: 4 (over z).
Axes of the slice: x: 2, y: 2, z: 4, core: 2. Of those that a mesh axis runs over, the one named last changes fastest.
Arguments:
- block_input: bfloat16 [4, 4, 1024, 1280], P(None, 'tensor', 'seq'), may hold values from -6 to 6
- cotangent: bfloat16 [4, 4, 1024, 1280], P(None, 'tensor', 'seq'), may hold values from -6 to 6
- mask: int32 [4, 4, 1024], P(None, 'tensor', 'seq'), may hold values 0 or 1
- conv_in: bfloat16 [2, 1280, 640], P('section', None, 'tensor'), may hold values from -0.15625 to 0.15625
- bias_in: bfloat16 [2, 640], P('section', 'tensor'), may hold values from -2 to 2
- conv_mid: bfloat16 [2, 5, 640, 640], P('section', None, None, 'tensor'), may hold values from -0.109375 to 0.109375
- bias_mid: bfloat16 [2, 640], P('section', 'tensor'), may hold values from -2 to 2
- conv_out: bfloat16 [2, 640, 1280], P('section', 'tensor'), may hold values from -0.25 to 0.25
- bias_out: bfloat16 [2, 1280], P('section', 'tensor'), may hold values from -2 to 2
- gain_first: bfloat16 [2, 1280], P('section', 'tensor'), may hold values from 0.5 to 1.5
- shift_first: bfloat16 [2, 1280], P('section', 'tensor'), may hold values from -2 to 2
- gain_second: bfloat16 [2, 640], P('section', 'tensor'), may hold values from 0.5 to 1.5
- shift_second: bfloat16 [2, 640], P('section', 'tensor'), may hold values from -2 to 2
- gain_third: bfloat16 [2, 640], P('section', 'tensor'), may hold values from 0.5 to 1.5
- shift_third: bfloat16 [2, 640], P('section', 'tensor'), may hold values from -2 to 2
Outputs:
- block_out: bfloat16 [2, 4, 4, 1024, 1280], P('section', None, 'tensor', 'seq')
- input_grad: bfloat16 [2, 4, 4, 1024, 1280], P('section', None, 'tensor', 'seq')
- grad_conv_in: float32 [2, 1280, 640], P('section', None, 'tensor')
- grad_bias_in: float32 [2, 640], P('section', 'tensor')
- grad_conv_mid: float32 [2, 5, 640, 640], P('section', None, None, 'tensor')
- grad_bias_mid: float32 [2, 640], P('section', 'tensor')
- grad_conv_out: float32 [2, 640, 1280], P('section', 'tensor')
- grad_bias_out: float32 [2, 1280], P('section', 'tensor')
- grad_gain_first: float32 [2, 1280], P('section', 'tensor')
- grad_shift_first: float32 [2, 1280], P('section', 'tensor')
- grad_gain_second: float32 [2, 640], P('section', 'tensor')
- grad_shift_second: float32 [2, 640], P('section', 'tensor')
- grad_gain_third: float32 [2, 640], P('section', 'tensor')
- grad_shift_third: float32 [2, 640], P('section', 'tensor')
All inputs are finite; a program needn't handle non-finite values. No bound on the sum of `mask` on one device may be relied on, other than what follows from the above.
Results may differ from a plain program's by a relative error of at most 0.012.
Values may be sent and summed in bfloat16 or wider, within the bound.
A program may use at most 256 MiB of HBM per device.

v0:
```python
import functools

import jax
import jax.numpy as jnp
from jax import lax
from jax.experimental import pallas as pl
from jax.experimental.pallas import tpu as pltpu
from jax.sharding import PartitionSpec as P

DILATION_BASE = 64
EPS = 1e-05
ROOT_HALF = 0.7071067811865476
INVERSE_ROOT_TWO_PI = 0.3989422804014327
MESH = pl.DeviceIdType.MESH
f32 = jnp.float32
bf16 = jnp.bfloat16

MICRO = 4
LEN = 256
H = 640
ROWS = MICRO * LEN
SHARDS = 4
PART = H // SHARDS
HALF = PART // 2
BLOCKS = 9
TILE = 256
WIDE = 128
X_STEP = 10
A_STEP = 8
LEAD = 3
NN = (((1,), (0,)), ((), ()))
NT = (((1,), (1,)), ((), ()))
TN = (((0,), (0,)), ((), ()))

E_AT, SX_AT, LV_AT, POOL_ROWS = 0, 2 * ROWS, 4 * ROWS, 6 * ROWS
KEEP_SLOTS, GIVE_SLOTS = 3, 3
SCHEDULE = (
    ("compute", 0, None),
    ("core", 1, None),
    ("y", 3, False),
    ("one", 3, False),
    ("one", 1, True),
    ("two", 5, False),
    ("two", 3, True),
    ("end", 8, False),
    ("end", 5, True),
    ("settle", 11, False),
    ("settle", 8, True),
    ("finish", 13, None),
)
LAST_LAG = 13


def dot(a, b, dims):
    return lax.dot_general(a, b, dims, preferred_element_type=f32)


def loop(count, body):
    def step(i, carry):
        body(i)
        return carry

    lax.fori_loop(0, count, step, 0)


def unroll(count, body):
    for i in range(count):
        body(i)


def row_stats(parts, width):
    mean = sum(jnp.sum(x, axis=-1, keepdims=True) for x in parts) / width
    spread = sum(jnp.sum(x * x, axis=-1, keepdims=True) for x in parts) / width - mean * mean
    return mean, lax.rsqrt(spread + EPS)


def gelu_slope(v):
    phi = 0.5 * (1.0 + lax.erf(v * ROOT_HALF))
    return phi, phi + v * (jnp.exp(-0.5 * v * v) * INVERSE_ROOT_TWO_PI)


def norm_back(ys, normeds, inverse, gains, width):
    scaled = [y * g for y, g in zip(ys, gains)]
    total = sum(jnp.sum(s, axis=-1, keepdims=True) for s in scaled) / width
    along = sum(jnp.sum(s * n, axis=-1, keepdims=True) for s, n in zip(scaled, normeds)) / width
    return [inverse * (s - total - n * along) for s, n in zip(scaled, normeds)]


def eights(x):
    return jnp.sum(x.reshape(x.shape[0] // 8, 8, x.shape[1]), axis=0)


def relay_kernel(fused, *refs):
    if fused:
        (xin, cot, mask, wsh, vsh, bo, ig, gout, vout) = refs[:9]
        rest = refs[9:]
    else:
        (xin, cot, mask, wfull, wother, v640_in, v1280_in, vx_in, bo, ig, gout, vout) = refs[:12]
        rest = refs[12:]
    (W, WX, POOL, A1, S1, A2, S2, N2, A3, S3, N3, U, GM, GH, XR, ST, TG, V640, V1280, VX, AC, VS) = rest[:22]
    (l_in, l_w, o_bo, o_ig, x_s, x_r, ha_s, ha_r, hg_s, hg_r) = rest[22:32]
    if fused:
        (VG, CR, KEEP, GIVE, YR, ZR, YX, VR, vg_s, vg_r, gz_s, gz_r, gy_s, gy_r, gc_s, gc_r, wx_s, wx_r, wc_s, wc_r, rc_s, rc_r, ry_s, ry_r, rz_s, rz_r, fy_s, fy_r, fc_s, fc_r, vr_s, vr_r, o_g) = rest[32:]
    else:
        (o_g,) = rest[32:]

    sec = lax.axis_index("section")
    seq = lax.axis_index("seq")
    ten = lax.axis_index("tensor")
    y = seq // 2
    core = lax.rem(seq, 2)
    at_core = (sec, y * 2 + (1 - core), ten)
    at_y = (sec, (1 - y) * 2 + core, ten)
    at_diag = (sec, (1 - y) * 2 + (1 - core), ten)
    at_x = (1 - sec, seq, ten)
    up, down = (sec, seq, ten + 1), (sec, seq, ten - 1)
    behind, ahead = (sec, seq - 1, ten), (sec, seq + 1, ten)
    first = sec == 0

    def remote(src, dst, send, recv, where):
        return pltpu.make_async_remote_copy(src_ref=src, dst_ref=dst, send_sem=send, recv_sem=recv, device_id=where, device_id_type=MESH)

    def rows(base, m, r=0, n=LEN):
        return pl.ds(pl.multiple_of(base + m * LEN + r, 16), n)

    def load_in(m, h, ref, into):
        return pltpu.make_async_copy(ref.at[m, :, pl.ds(h * H, H)], into, l_in.at[m, h, 0 if ref is xin else 1])

    for m in range(MICRO):
        for h in range(2):
            load_in(m, h, xin, POOL.at[pl.ds(E_AT + h * ROWS + m * LEN, LEN), :]).start()
            load_in(m, h, cot, U.at[h, pl.ds(m * LEN, LEN), :]).start()
    if fused:
        own_w = pltpu.make_async_copy(wsh, W.at[:, pl.ds(pl.multiple_of(ten * PART, 16), PART), :], l_w.at[0])
        own_v = pltpu.make_async_copy(vsh, VG.at[sec, ten], l_w.at[1])
        own_w.start()
        own_v.start()
        partners = [at_core, at_y, at_diag]
        others = [(s, d) for s in range(2) for d in range(SHARDS) if s or d]
        partners += [(lax.rem(sec + s, 2), seq, lax.rem(ten + d, SHARDS)) for s, d in others]
    else:
        own_w = pltpu.make_async_copy(wfull, W, l_w.at[0])
        own_v = pltpu.make_async_copy(wother, WX, l_w.at[1])
        own_w.start()
        own_v.start()
        partners = [at_core, at_diag, at_x]

    barrier = pltpu.get_barrier_semaphore()
    for partner in partners:
        pl.semaphore_signal(barrier, inc=1, device_id=partner, device_id_type=MESH)
    pl.semaphore_wait(barrier, len(partners))

    def piece(ref, b, s, half):
        return ref.at[b, pl.ds(pl.multiple_of(s * PART + half * HALF, 16), HALF), :]

    def gz(b, s, to_up, src=None):
        spot = piece(W, b, s, core)
        return remote(spot if src is None else src, spot, gz_s.at[b, s, 0 if to_up else 1], gz_r.at[b, s], up if to_up else down)

    def gy(b, s):
        spot = piece(W, b, s, core)
        return remote(spot, spot, gy_s.at[b, s], gy_r.at[b, s], at_y)

    def gc(b, s, half):
        spot = piece(W, b, s, half)
        return remote(spot, spot, gc_s.at[b, s], gc_r.at[b, s], at_core)

    def wanted(b):
        return b // 2 == sec

    def gx(b, s, src=None):
        k = lax.rem(b, 2)
        return remote(piece(W, b, s, core) if src is None else src, piece(WX, k, s, core), wx_s.at[k, s], wx_r.at[k, s], at_x)

    def gxc(k, s, half):
        spot = piece(WX, k, s, half)
        return remote(spot, spot, wc_s.at[k, s], wc_r.at[k, s], at_core)

    mine = lambda b: jnp.logical_or(b == BLOCKS - 1, lax.rem(b, 2) == y)
    def send_own(b):
        src = wsh.at[b, pl.ds(pl.multiple_of(core * HALF, 16), HALF), :]

        @pl.when(jnp.logical_and(mine(b), ten < SHARDS - 1))
        def _():
            gz(b, ten, True, src).start()

        @pl.when(jnp.logical_and(mine(b), ten > 0))
        def _():
            gz(b, ten, False, src).start()

        @pl.when(wanted(b))
        def _():
            gx(b, ten, src).start()

    def gather_begin():
        for i, (s, d) in enumerate(others):
            remote(vsh, VG.at[sec, ten], vg_s.at[i], vg_r.at[i], (lax.rem(sec + s, 2), seq, lax.rem(ten + d, SHARDS))).start()
        for b in range(LEAD):
            send_own(b)

    def gather_step(k):
        @pl.when(k + LEAD < BLOCKS)
        def _():
            send_own(k + LEAD)

        for d in range(1, SHARDS):
            b = k - (d - 1)
            ok = jnp.logical_and(b >= 0, b < BLOCKS)
            for above in (False, True):
                s = ten + d if above else ten - d
                there = jnp.logical_and(ok, s < SHARDS if above else s >= 0)
                onward = (ten > 0) if above else (ten < SHARDS - 1)

                @pl.when(jnp.logical_and(there, mine(b)))
                def _():
                    gz(b, s, True).wait_recv()

                    @pl.when(onward)
                    def _():
                        gz(b, s, not above).start()

                    @pl.when(b < BLOCKS - 1)
                    def _():
                        gy(b, s).start()

                    gc(b, s, core).start()

                    @pl.when(wanted(b))
                    def _():
                        gx(b, s).start()

        for d in range(1, SHARDS):
            b = k - d
            ok = jnp.logical_and(b >= 0, b < BLOCKS)
            for above in (False, True):
                s = ten + d if above else ten - d
                there = jnp.logical_and(ok, s < SHARDS if above else s >= 0)

                @pl.when(jnp.logical_and(there, jnp.logical_not(mine(b))))
                def _():
                    gy(b, s).wait_recv()
                    gc(b, s, core).start()

                    @pl.when(wanted(b))
                    def _():
                        gx(b, s).start()

        b = k - 4
        for s in range(SHARDS):

            @pl.when(jnp.logical_and(jnp.logical_and(b >= 0, b < BLOCKS), s != ten))
            def _():
                gc(b, s, 1 - core).wait_recv()

        @pl.when(jnp.logical_and(k >= X_STEP, k < X_STEP + 2))
        def _():
            for s in range(SHARDS):
                gx(k - X_STEP, s).wait_recv()
                gxc(k - X_STEP, s, core).start()

    def others_blocks():
        for k in range(2):
            for s in range(SHARDS):
                gxc(k, s, 1 - core).wait_recv()

    def gather_drain(b):
        @pl.when(b < 2)
        def _():
            for s in range(SHARDS):
                gx(b, s).wait_send()
                gxc(b, s, core).wait_send()

        for s in range(SHARDS):
            fromabove = s > ten

            @pl.when(jnp.logical_and(mine(b), jnp.logical_and(s <= ten, ten < SHARDS - 1)))
            def _():
                gz(b, s, True).wait_send()

            @pl.when(jnp.logical_and(mine(b), jnp.logical_and(s >= ten, ten > 0)))
            def _():
                gz(b, s, False).wait_send()

            @pl.when(s != ten)
            def _():
                gc(b, s, core).wait_send()

                @pl.when(jnp.logical_and(mine(b), b < BLOCKS - 1))
                def _():
                    gy(b, s).wait_send()

    def vectors():
        own_v.wait()
        for i, (s, d) in enumerate(others):
            remote(vsh, VG.at[sec, ten], vg_s.at[i], vg_r.at[i], at_x).wait()
        line = lax.broadcasted_iota(jnp.int32, (2 * 128, H), 0)
        col = lax.broadcasted_iota(jnp.int32, (2 * 128, H), 1)

        def pick(offset):
            return jnp.where(col == line + offset, 1.0, 0.0).astype(bf16)

        narrow = jnp.zeros((16, H), f32)
        wide = [[jnp.zeros((16, H), f32) for _ in range(4)] for _ in range(2)]
        for s in range(SHARDS):
            inner = pick(s * PART)
            narrow = narrow + dot(VG[sec, s], inner, NN)
            for who in range(2):
                held = VG[sec if who == 0 else 1 - sec, s]
                for h in range(2):
                    for k in range(2):
                        put = pick(s * 2 * PART + k * PART - h * H)
                        wide[who][h * 2 + k] = wide[who][h * 2 + k] + dot(held, put, NN)
        V640[...] = narrow
        for who, into in ((0, V1280), (1, VX)):
            for h in range(2):
                into[h, 0:3, :] = wide[who][h * 2][6:9] + wide[who][h * 2 + 1][9:12]

    def halo(ref, sends, recvs, m, reach, start):
        fwd = remote(ref.at[m, pl.ds(2 * LEN - reach, reach), :], ref.at[m, pl.ds(LEN - reach, reach), :], sends.at[m, 0], recvs.at[m, 0], ahead)
        bwd = remote(ref.at[m, pl.ds(LEN, reach), :], ref.at[m, pl.ds(2 * LEN, reach), :], sends.at[m, 1], recvs.at[m, 1], behind)

        @pl.when(seq < 3)
        def _():
            fwd.start() if start else fwd.wait_send()

        @pl.when(seq > 0)
        def _():
            bwd.start() if start else bwd.wait_send()

        if not start:

            @pl.when(seq > 0)
            def _():
                fwd.wait_recv()

            @pl.when(seq < 3)
            def _():
                bwd.wait_recv()

    def x_send(m, src):
        return remote(src.at[rows(0, m), :], XR.at[rows(0, m), :], x_s.at[m], x_r.at[m], at_x)

    def stage_first(m):
        def tile(i):
            r = i * WIDE
            at = rows(0, m, r, WIDE)
            x = [POOL[rows(E_AT + h * ROWS, m, r, WIDE), :].astype(f32) for h in range(2)]
            mean, inverse = row_stats(x, 2 * H)
            ST[at, 0:1] = mean
            ST[at, 1:2] = inverse
            for h in range(2):
                v = (x[h] - mean) * inverse * V1280[h, 1:2, :] + V1280[h, 2:3, :]
                phi, slope = gelu_slope(v)
                A1[h, at, :] = (v * phi).astype(bf16)
                S1[h, at, :] = slope.astype(bf16)

        unroll(LEN // WIDE, tile)

    def stage_a(m, reach):
        here = rows(0, m)
        TG[0:LEN, :] = dot(A1[0, here, :], W[2], NT) + dot(A1[1, here, :], W[3], NT)

        def tile2(i):
            r = i * TILE
            at = rows(0, m, r, TILE)
            x = TG[pl.ds(r, TILE), :] + V640[0:1, :]
            mean, inverse = row_stats([x], H)
            normed = (x - mean) * inverse
            v = normed * V640[2:3, :] + V640[3:4, :]
            phi, slope = gelu_slope(v)
            A2[m, pl.ds(pl.multiple_of(LEN + r, 16), TILE), :] = (v * phi).astype(bf16)
            S2[at, :] = slope.astype(bf16)
            N2[at, :] = normed.astype(bf16)
            ST[at, 2:3] = inverse

        unroll(LEN // TILE, tile2)
        halo(A2, ha_s, ha_r, m, reach, True)

    def stage_b(m, span, relay):
        halo(A2, ha_s, ha_r, m, 2 * span, False)
        TG[0:LEN, :] = sum(dot(A2[m, pl.ds(LEN + (t - 2) * span, LEN), :], W[4 + t], NT) for t in (2, 0, 1, 3, 4))

        def tile(i):
            r = i * TILE
            at = rows(0, m, r, TILE)
            x = TG[pl.ds(r, TILE), :] + V640[1:2, :]
            mean, inverse = row_stats([x], H)
            normed = (x - mean) * inverse
            v = normed * V640[4:5, :] + V640[5:6, :]
            phi, slope = gelu_slope(v)
            A3[at, :] = (v * phi).astype(bf16)
            S3[at, :] = slope.astype(bf16)
            N3[at, :] = normed.astype(bf16)
            ST[at, 3:4] = inverse

        unroll(LEN // TILE, tile)
        if relay:
            x_send(m, A3).start()
        here = rows(0, m)
        for h in range(2):
            mixed = dot(A3[here, :], W[h], NN) + V1280[h, 0:1, :]
            POOL[rows(LV_AT + h * ROWS, m), :] = (POOL[rows(E_AT + h * ROWS, m), :].astype(f32) + mixed).astype(bf16)
            out_bo(m, h).start()

    def out_bo(m, h):
        return pltpu.make_async_copy(POOL.at[rows(LV_AT + h * ROWS, m), :], bo.at[m, :, pl.ds(h * H, H)], o_bo.at[m, h])

    def out_ig(m, h):
        return pltpu.make_async_copy(S1.at[h, rows(0, m), :], ig.at[m, :, pl.ds(h * H, H)], o_ig.at[m, h])

    def stage_x(m):
        x_send(m, A3).wait_recv()
        for h in range(2):
            at = rows(E_AT + h * ROWS, m)
            mixed = dot(XR[rows(0, m), :], WX[h], NN) + VX[h, 0:1, :]
            POOL[at, :] = (POOL[at, :].astype(f32) + mixed).astype(bf16)

    def stage_n(m):
        def tile(i):
            r = i * WIDE
            at = rows(0, m, r, WIDE)
            x = [POOL[rows(LV_AT + h * ROWS, m, r, WIDE), :].astype(f32) for h in range(2)]
            mean, inverse = row_stats(x, 2 * H)
            ST[at, 4:5] = mean
            ST[at, 5:6] = inverse
            for h in range(2):
                v = (x[h] - mean) * inverse * VX[h, 1:2, :] + VX[h, 2:3, :]
                POOL[rows(SX_AT + h * ROWS, m, r, WIDE), :] = gelu_slope(v)[1].astype(bf16)

        unroll(LEN // WIDE, tile)

    def stage_q(m):
        x_send(m, GH).wait_recv()
        for h in range(2):
            TG[h * LEN : (h + 1) * LEN, :] = dot(XR[rows(0, m), :], WX[h], NN)

        def tile(i):
            r = i * WIDE
            at = rows(0, m, r, WIDE)
            mean, inverse = ST[at, 4:5], ST[at, 5:6]
            ys, normeds = [], []
            for h in range(2):
                slope = POOL[rows(SX_AT + h * ROWS, m, r, WIDE), :].astype(f32)
                ys.append(TG[pl.ds(h * LEN + r, WIDE), :] * slope)
                normeds.append((POOL[rows(LV_AT + h * ROWS, m, r, WIDE), :].astype(f32) - mean) * inverse)
            grads = norm_back(ys, normeds, inverse, [VX[h, 1:2, :] for h in range(2)], 2 * H)
            for h in range(2):
                U[h, at, :] = (U[h, at, :].astype(f32) + grads[h]).astype(bf16)

        unroll(LEN // WIDE, tile)

    def back_three(m):
        here = rows(0, m)
        TG[LEN : 2 * LEN, :] = dot(U[0, here, :], W[0], NT) + dot(U[1, here, :], W[1], NT)

    def stage_p1(m, reach):
        back_three(m)

        def tile(i):
            r = i * TILE
            at = rows(0, m, r, TILE)
            y_ = TG[pl.ds(LEN + r, TILE), :] * S3[at, :].astype(f32)
            normed = N3[at, :].astype(f32)
            (grad,) = norm_back([y_], [normed], ST[at, 3:4], [V640[4:5, :]], H)
            low = grad.astype(bf16)
            GM[m, pl.ds(pl.multiple_of(LEN + r, 16), TILE), :] = low
            AC[4] += eights(y_ * normed)
            AC[5] += eights(y_)
            AC[1] += eights(low.astype(f32))
            for h in range(2):
                AC[6 + h] += eights(U[h, at, :].astype(f32))

        unroll(LEN // TILE, tile)
        halo(GM, hg_s, hg_r, m, reach, True)

    def stage_p2(m, span, relay):
        halo(GM, hg_s, hg_r, m, 2 * span, False)
        TG[0:LEN, :] = sum(dot(GM[m, pl.ds(LEN - (t - 2) * span, LEN), :], W[4 + t], NN) for t in (2, 0, 1, 3, 4))

        def tile(i):
            r = i * TILE
            at = rows(0, m, r, TILE)
            y_ = TG[pl.ds(r, TILE), :] * S2[at, :].astype(f32)
            normed = N2[at, :].astype(f32)
            (grad,) = norm_back([y_], [normed], ST[at, 2:3], [V640[2:3, :]], H)
            low = grad.astype(bf16)
            GH[at, :] = low
            AC[2] += eights(y_ * normed)
            AC[3] += eights(y_)
            AC[0] += eights(low.astype(f32))

        unroll(LEN // TILE, tile)
        if relay:
            x_send(m, GH).start()

    def stage_p3(m):
        for h in range(2):
            TG[h * LEN : (h + 1) * LEN, :] = dot(GH[rows(0, m), :], W[2 + h], NN)

        def tile(i):
            r = i * WIDE
            at = rows(0, m, r, WIDE)
            mean, inverse = ST[at, 0:1], ST[at, 1:2]
            ys, normeds = [], []
            for h in range(2):
                ys.append(TG[pl.ds(h * LEN + r, WIDE), :] * S1[h, at, :].astype(f32))
                normeds.append((POOL[rows(E_AT + h * ROWS, m, r, WIDE), :].astype(f32) - mean) * inverse)
            grads = norm_back(ys, normeds, inverse, [V1280[h, 1:2, :] for h in range(2)], 2 * H)
            for h in range(2):
                S1[h, at, :] = (U[h, at, :].astype(f32) + grads[h]).astype(bf16)
                AC[8 + h] += eights(ys[h] * normeds[h])
                AC[10 + h] += eights(ys[h])

        unroll(LEN // WIDE, tile)
        for h in range(2):
            out_ig(m, h).start()

    def prepare():
        AC[...] = jnp.zeros_like(AC)
        for ref in (A2, GM):

            @pl.when(seq == 0)
            def _():
                for m in range(MICRO):
                    ref[m, 0:LEN, :] = jnp.zeros((LEN, H), bf16)

            @pl.when(seq == 3)
            def _():
                for m in range(MICRO):
                    ref[m, 2 * LEN : 3 * LEN, :] = jnp.zeros((LEN, H), bf16)

        for m in range(MICRO):
            ST[m * LEN : (m + 1) * LEN, 6:7] = jnp.transpose(jnp.broadcast_to(mask[m : m + 1, :].astype(f32), (128, LEN)))[:, 0:1]
        for m in range(MICRO):
            for h in range(2):
                load_in(m, h, xin, POOL.at[pl.ds(E_AT + h * ROWS + m * LEN, LEN), :]).wait()
                load_in(m, h, cot, U.at[h, pl.ds(m * LEN, LEN), :]).wait()

        def masked(m):
            at = rows(0, m)
            keep = ST[at, 6:7]
            for h in range(2):
                U[h, at, :] = (U[h, at, :].astype(f32) * keep).astype(bf16)

        loop(MICRO, masked)

    SPAN_0, SPAN_1 = DILATION_BASE, 2 * DILATION_BASE
    span = DILATION_BASE * (1 + sec)
    early = 0
    if fused:
        gather_begin()
        prepare()
        own_w.wait()
        vectors()
        early = MICRO

        def step(k):
            gather_step(k)

            @pl.when(jnp.logical_and(first, jnp.logical_and(k >= 1, k < 1 + MICRO)))
            def _():
                stage_first(k - 1)

            @pl.when(jnp.logical_and(first, jnp.logical_and(k >= A_STEP, k < A_STEP + MICRO)))
            def _():
                stage_a(k - A_STEP, 2 * SPAN_0)

        loop(BLOCKS + 4, step)
    else:
        own_w.wait()
        own_v.wait()
        for src, dst in ((v640_in, V640), (v1280_in, V1280), (vx_in, VX)):
            dst[...] = src[...]
        prepare()

    @pl.when(first)
    def _():
        def firsts(m):
            stage_first(m)
            stage_a(m, 2 * SPAN_0)

        if early == 0:
            loop(MICRO, firsts)
        loop(MICRO, lambda m: stage_b(m, SPAN_0, True))
        if fused:
            others_blocks()
        loop(MICRO, stage_n)

        def backward(m):
            stage_q(m)
            stage_p1(m, 2 * SPAN_0)

            @pl.when(m > 0)
            def _():
                stage_p3(m - 1)

            @pl.when(m < MICRO - 1)
            def _():
                stage_p2(m, SPAN_0, False)

        loop(MICRO, backward)

    @pl.when(jnp.logical_not(first))
    def _():
        if fused:
            others_blocks()

        def both(k):
            @pl.when(k == MICRO + 1)
            def _():
                loop(MICRO - 1, stage_p3)

            @pl.when(k < MICRO)
            def _():
                stage_x(k)
                stage_first(k)
                stage_a(k, 2 * SPAN_1)

            inner = jnp.logical_and(k >= 1, k <= MICRO)

            @pl.when(inner)
            def _():
                stage_b(k - 1, SPAN_1, False)

            @pl.when(k >= 2)
            def _():
                stage_p2(k - 2, SPAN_1, True)

            @pl.when(inner)
            def _():
                stage_p1(k - 1, 2 * SPAN_1)

        loop(MICRO + 2, both)

    def last_grad_hidden():
        @pl.when(first)
        def _():
            stage_p2(MICRO - 1, SPAN_0, False)

    def last_input_grad():
        stage_p3(MICRO - 1)
        for i in range(12):
            VS[0, i : i + 1, :] = jnp.sum(AC[i], axis=0, keepdims=True)
        VS[0, 12:16, :] = jnp.zeros((4, H), f32)

    def relay_drain():
        loop(MICRO, lambda m: x_send(m, A3).wait_send())

        def out_wait(m):
            for h in range(2):
                out_bo(m, h).wait()
                out_ig(m, h).wait()

        loop(MICRO, out_wait)

    def gradient(b):
        @pl.when(b < 2)
        def _():
            TG[...] = dot(A3[...], U[b], TN)

        @pl.when(jnp.logical_and(b >= 2, b < 4))
        def _():
            TG[...] = dot(GH[...], A1[b - 2], TN)

        @pl.when(b >= 4)
        def _():
            at = pl.ds(pl.multiple_of(LEN + (b - 6) * span, 64), LEN)
            TG[...] = sum(dot(GM[m, LEN : 2 * LEN, :], A2[m, at, :], TN) for m in range(MICRO))

    if not fused:
        last_grad_hidden()
        last_input_grad()
        relay_drain()

        def whole(b):
            gradient(b)
            out = pltpu.make_async_copy(TG, gout.at[b], o_g.at[b])
            out.start()
            out.wait()

        loop(BLOCKS, whole)
        vout[...] = VS[0]
        return

    kind = lambda p: lax.rem(p + 2, 3)
    slot = lambda p: p // 3
    over_tensor_first = lambda p: kind(p) == 2
    zslot = lambda p: slot(p) + jnp.where(over_tensor_first(p), 3, 0)
    owned = lambda p: jnp.logical_or(over_tensor_first(p), kind(p) == y)
    block = lambda p: jnp.where(p < 2, p, jnp.where(p < 7, p + 2, p - 5))
    outer = jnp.logical_or(ten == 0, ten == SHARDS - 1)
    low_side = ten < SHARDS // 2
    FAR, NEAR = jnp.where(low_side, 3, 0), jnp.where(low_side, 2, 1)

    def half_of(half):
        return pl.ds(pl.multiple_of(half * HALF, 16), HALF)

    def part(p, s):
        return CR.at[p, pl.ds(pl.multiple_of(s * HALF, 16), HALF), :]

    def kept(p, s):
        return KEEP.at[lax.rem(p, KEEP_SLOTS), s * HALF : (s + 1) * HALF, :]

    def final(p, half):
        return gout.at[block(p), half_of(half), :]

    def rc(p):
        return remote(GIVE.at[lax.rem(p, GIVE_SLOTS)], CR.at[p], rc_s.at[p], rc_r.at[p], at_core)

    def ry(p, s):
        return remote(part(p, s), YR.at[slot(p), s], ry_s.at[slot(p), s], ry_r.at[slot(p), s], at_y)

    def rz(p, s, idx_send, idx, to):
        return remote(part(p, s), ZR.at[zslot(p), idx], rz_s.at[zslot(p), idx_send], rz_r.at[zslot(p), idx], (sec, seq, to))

    def fy(p, into):
        return remote(part(p, ten), into, fy_s.at[p], fy_r.at[p], at_y)

    def fc(p, src, half):
        return remote(src, final(p, half), fc_s.at[p], fc_r.at[p], at_core)

    def out_g(p):
        return pltpu.make_async_copy(part(p, ten), final(p, core), o_g.at[p])

    def add(ref, *others_):
        total = ref[...].astype(f32)
        for other in others_:
            total = total + other[...].astype(f32)
        ref[...] = total.astype(bf16)

    def compute(p):
        @pl.when(p >= GIVE_SLOTS)
        def _():
            rc(p - GIVE_SLOTS).wait_send()

        gradient(block(p))
        for s in range(SHARDS):
            theirs = TG[pl.ds(pl.multiple_of(s * PART + (1 - core) * HALF, 16), HALF), :]
            GIVE[lax.rem(p, GIVE_SLOTS), s * HALF : (s + 1) * HALF, :] = theirs.astype(bf16)
        rc(p).start()
        for s in range(SHARDS):
            kept(p, s)[...] = TG[pl.ds(pl.multiple_of(s * PART + core * HALF, 16), HALF), :].astype(bf16)

    def over_core(p):
        rc(p).wait_recv()
        for s in (0, 3, 1, 2):
            add(part(p, s), kept(p, s))

            @pl.when(jnp.logical_not(owned(p)))
            def _():
                ry(p, s).start()

    def over_y(p):
        @pl.when(owned(p))
        def _():
            for s in (0, 3, 1, 2):
                ry(p, s).wait_recv()
                add(part(p, s), YR.at[slot(p), s])

    def chain_one(p):
        @pl.when(jnp.logical_and(owned(p), outer))
        def _():
            for k in range(3):
                s = jnp.where(low_side, 3 - k, k)
                idx = jnp.where(low_side, s - 1, s)
                rz(p, s, idx, idx, jnp.where(low_side, 1, 2)).start()

        @pl.when(jnp.logical_and(owned(p), jnp.logical_not(outer)))
        def _():
            s = jnp.where(low_side, 0, 3)
            rz(p, s, 0, 0, s).start()

    def chain_two(p):
        @pl.when(jnp.logical_and(owned(p), jnp.logical_not(outer)))
        def _():
            for s, idx, idx_send in ((FAR, jnp.where(low_side, 2, 0), 1), (NEAR, 1, 2)):
                rz(p, s, idx_send, idx, s).wait_recv()
                add(part(p, s), ZR.at[zslot(p), idx])
                rz(p, s, idx_send, 3, s).start()

    def chain_end(p):
        @pl.when(owned(p))
        def _():
            idx = jnp.where(ten == 2, 2, 0)
            rz(p, ten, 0, idx, ten).wait_recv()
            rz(p, ten, 0, 3, ten).wait_recv()
            add(part(p, ten), ZR.at[zslot(p), idx], ZR.at[zslot(p), 3])

            @pl.when(over_tensor_first(p))
            def _():
                fy(p, YX.at[slot(p)]).start()

            @pl.when(jnp.logical_not(over_tensor_first(p)))
            def _():
                fy(p, final(p, core)).start()
                fc(p, part(p, ten), core).start()
                out_g(p).start()

    def settle(p):
        @pl.when(over_tensor_first(p))
        def _():
            fy(p, YX.at[slot(p)]).wait()
            add(part(p, ten), YX.at[slot(p)])
            fc(p, part(p, ten), core).start()
            out_g(p).start()

        @pl.when(jnp.logical_not(owned(p)))
        def _():
            fy(p, final(p, core)).wait_recv()
            fc(p, final(p, core), core).start()

    def finish(p):
        fc(p, part(p, ten), 1 - core).wait_recv()

    def vector_round(i):
        pair, far = ten + 1 - 2 * lax.rem(ten, 2), lax.rem(ten + 2, SHARDS)
        where_seq = jnp.where(i == 0, y * 2 + 1 - core, jnp.where(i == 1, (1 - y) * 2 + core, seq))
        where_ten = jnp.where(i == 2, pair, jnp.where(i == 3, far, ten))
        return remote(VS.at[i], VR.at[i], vr_s.at[i], vr_r.at[i], (sec, where_seq, where_ten))

    def sums(t):
        for stage, lag, first_kind in SCHEDULE:
            p = t - lag
            fits = jnp.logical_and(p >= 0, p < BLOCKS)
            if first_kind is not None:
                fits = jnp.logical_and(fits, over_tensor_first(p) if first_kind else jnp.logical_not(over_tensor_first(p)))
            if stage == "compute":

                @pl.when(p == BLOCKS - 2)
                def _():
                    last_grad_hidden()

            @pl.when(fits)
            def _():
                dict(compute=compute, core=over_core, y=over_y, one=chain_one, two=chain_two, end=chain_end, settle=settle, finish=finish)[stage](p)

        @pl.when(t == BLOCKS)
        def _():
            last_input_grad()

        i = t - BLOCKS - 1

        @pl.when(jnp.logical_and(i > 0, i <= 4))
        def _():
            vector_round(i - 1).wait()
            VS[i] = VS[i - 1] + VR[i - 1]

        @pl.when(jnp.logical_and(i >= 0, i < 4))
        def _():
            vector_round(i).start()

    loop(BLOCKS + LAST_LAG, sums)
    vout[...] = VS[4]

    relay_drain()
    loop(BLOCKS, gather_drain)

    def drain(p):
        @pl.when(p >= BLOCKS - GIVE_SLOTS)
        def _():
            rc(p).wait_send()

        fc(p, part(p, ten), core).wait_send()

        @pl.when(owned(p))
        def _():
            out_g(p).wait()

            @pl.when(jnp.logical_not(over_tensor_first(p)))
            def _():
                fy(p, final(p, core)).wait_send()

            for k in range(3):
                rz(p, ten, k, 0, ten).wait_send()

        @pl.when(jnp.logical_not(owned(p)))
        def _():
            for s in range(SHARDS):
                ry(p, s).wait_send()

    loop(BLOCKS, drain)


def relay(block_input, cotangent, mask, weights, vectors, fused):
    hbm = pl.BlockSpec(memory_space=pl.ANY)
    vmem = pl.BlockSpec(memory_space=pltpu.VMEM)
    dma = lambda *shape: pltpu.SemaphoreType.DMA(shape)
    low = lambda *shape: pltpu.VMEM(shape, bf16)
    full = lambda *shape: pltpu.VMEM(shape, f32)
    scratch = [
        low(BLOCKS, H, H),
        low(2, H, H),
        low(POOL_ROWS, H),
        low(2, ROWS, H),
        low(2, ROWS, H),
        low(MICRO, 3 * LEN, H),
        low(ROWS, H),
        low(ROWS, H),
        low(ROWS, H),
        low(ROWS, H),
        low(ROWS, H),
        low(2, ROWS, H),
        low(MICRO, 3 * LEN, H),
        low(ROWS, H),
        low(ROWS, H),
        full(ROWS, 8),
        full(H, H),
        full(16, H),
        full(2, 8, H),
        full(2, 8, H),
        full(12, 8, H),
        full(5, 16, H),
        dma(MICRO, 2, 2),
        dma(2),
        dma(MICRO, 2),
        dma(MICRO, 2),
        dma(MICRO),
        dma(MICRO),
        dma(MICRO, 2),
        dma(MICRO, 2),
        dma(MICRO, 2),
        dma(MICRO, 2),
    ]
    if fused:
        scratch += [
            low(2, SHARDS, 16, 256),
            low(BLOCKS, SHARDS * HALF, H),
            low(KEEP_SLOTS, SHARDS * HALF, H),
            low(GIVE_SLOTS, SHARDS * HALF, H),
            low(3, SHARDS, HALF, H),
            low(6, 4, HALF, H),
            low(3, HALF, H),
            full(4, 16, H),
            dma(7),
            dma(7),
            dma(BLOCKS, SHARDS, 2),
            dma(BLOCKS, SHARDS),
            dma(BLOCKS, SHARDS),
            dma(BLOCKS, SHARDS),
            dma(BLOCKS, SHARDS),
            dma(BLOCKS, SHARDS),
            dma(2, SHARDS),
            dma(2, SHARDS),
            dma(2, SHARDS),
            dma(2, SHARDS),
            dma(BLOCKS),
            dma(BLOCKS),
            dma(3, SHARDS),
            dma(3, SHARDS),
            dma(6, 3),
            dma(6, 4),
            dma(BLOCKS),
            dma(BLOCKS),
            dma(BLOCKS),
            dma(BLOCKS),
            dma(4),
            dma(4),
        ]
    scratch += [dma(BLOCKS)]
    outs = (
        jax.ShapeDtypeStruct((MICRO, LEN, 2 * H), bf16),
        jax.ShapeDtypeStruct((MICRO, LEN, 2 * H), bf16),
        jax.ShapeDtypeStruct((BLOCKS, PART, H), bf16) if fused else jax.ShapeDtypeStruct((BLOCKS, H, H), f32),
        jax.ShapeDtypeStruct((16, H), f32),
    )
    in_specs = [hbm, hbm, vmem] + [hbm] * len(weights) + ([hbm] if fused else [vmem] * 3)
    return pl.pallas_call(
        functools.partial(relay_kernel, fused),
        out_shape=outs,
        in_specs=in_specs,
        out_specs=(hbm, hbm, hbm, vmem),
        scratch_shapes=scratch,
        compiler_params=pltpu.CompilerParams(collective_id=0, has_side_effects=True, vmem_limit_bytes=62 * 2**20),
        cost_estimate=pl.CostEstimate(flops=25_000_000_000, bytes_accessed=20_000_000, transcendentals=4_000_000),
        name="relay",
    )(block_input, cotangent, mask, *weights, *vectors)


def packed_weights(conv_in, conv_mid, conv_out):
    channels = conv_out.shape[0]
    halves = lambda m: m.reshape(channels, 2, H).transpose(1, 0, 2)
    return jnp.concatenate([halves(conv_out), halves(conv_in.T), conv_mid.transpose(0, 2, 1)])


def local(*args):
    block_input, cotangent, mask = args[:3]
    (conv_in, bias_in, conv_mid, bias_mid, conv_out, bias_out, gain_first, shift_first, gain_second, shift_second, gain_third, shift_third) = (a[0] for a in args[3:])
    ten, sec = lax.axis_index("tensor"), lax.axis_index("section")
    shards = lax.axis_size("tensor")
    fused = shards == SHARDS
    channels = conv_out.shape[0]
    xin = block_input.reshape(MICRO, LEN, 2 * H)
    cot = cotangent.reshape(MICRO, LEN, 2 * H)
    mask = mask.reshape(MICRO, LEN)
    mine = packed_weights(conv_in, conv_mid, conv_out)
    narrow = (bias_in, bias_mid, gain_second, shift_second, gain_third, shift_third)
    wide = (bias_out, gain_first, shift_first)
    if fused:
        lines = jnp.stack(list(narrow) + [w[:PART] for w in wide] + [w[PART:] for w in wide])
        vsh = jnp.pad(lines, ((0, 4), (0, 256 - PART)))
        block_out, input_grad, grads, small = relay(xin, cot, mask, (mine,), (vsh,), True)
        grads = grads.astype(f32)
    else:
        whole = lax.all_gather(mine, "tensor", axis=1, tiled=True)
        swap = [(0, 1), (1, 0)]
        give = jnp.where(sec == 0, whole[0:2], whole[2:4])
        other = lax.ppermute(give, "section", swap)
        v_narrow = lax.all_gather(jnp.stack(narrow), "tensor", axis=1, tiled=True)
        v_wide = lax.all_gather(jnp.stack(wide), "tensor", axis=1, tiled=True)
        v640 = jnp.pad(v_narrow.astype(f32), ((0, 10), (0, 0)))
        v1280 = jnp.pad(v_wide.astype(f32).reshape(3, 2, H).transpose(1, 0, 2), ((0, 0), (0, 5), (0, 0)))
        vx = lax.ppermute(v1280, "section", swap)
        block_out, input_grad, grads, small = relay(xin, cot, mask, (whole, other), (v640, v1280, vx), False)
        grads = lax.psum(lax.psum_scatter(grads, "tensor", scatter_dimension=1, tiled=True), "seq")
        small = lax.psum(small, ("seq", "tensor"))
    grad_in = grads[2:4].transpose(0, 2, 1).reshape(2 * H, channels)
    grad_out = grads[0:2].transpose(1, 0, 2).reshape(channels, 2 * H)
    grad_mid = grads[4:9].transpose(0, 2, 1)
    thin = lax.dynamic_slice_in_dim(small[0:6], ten * channels, channels, 1)
    thick = lax.dynamic_slice_in_dim(small[6:12].reshape(3, 2 * H), ten * 2 * channels, 2 * channels, 1)
    shape = (1, MICRO, 1, LEN, 2 * H)
    return (
        block_out.reshape(shape),
        input_grad.reshape(shape),
        grad_in[None],
        thin[0:1],
        grad_mid[None],
        thin[1:2],
        grad_out[None],
        thick[0:1],
        thick[1:2],
        thick[2:3],
        thin[2:3],
        thin[3:4],
        thin[4:5],
        thin[5:6],
    )


def solution(mesh):
    in_specs = (
        P(None, "tensor", "seq", None),
        P(None, "tensor", "seq", None),
        P(None, "tensor", "seq"),
        P("section", None, "tensor"),
        P("section", "tensor"),
        P("section", None, None, "tensor"),
        P("section", "tensor"),
        P("section", "tensor", None),
        P("section", "tensor"),
        P("section", "tensor"),
        P("section", "tensor"),
        P("section", "tensor"),
        P("section", "tensor"),
        P("section", "tensor"),
        P("section", "tensor"),
    )
    out_specs = (
        P("section", None, "tensor", "seq", None),
        P("section", None, "tensor", "seq", None),
        P("section", None, "tensor"),
        P("section", "tensor"),
        P("section", None, None, "tensor"),
        P("section", "tensor"),
        P("section", "tensor", None),
        P("section", "tensor"),
        P("section", "tensor"),
        P("section", "tensor"),
        P("section", "tensor"),
        P("section", "tensor"),
        P("section", "tensor"),
        P("section", "tensor"),
    )
    return jax.shard_map(local, mesh=mesh, in_specs=in_specs, out_specs=out_specs, check_vma=False)
```

profile of v0, /device:TPU:0, one launch (start us, length us, event | category | flops | bytes accessed | tf_op | source)
XLA Modules:
  0.0 217.6 jit_solution(12161239309511380288)
XLA Ops:
  0.6 0.0 copy-start.1
  0.7 0.9 fusion.5
  1.5 1.3 copy.44
  2.8 0.8 fusion.3
  3.6 0.8 stack.2
  4.4 0.6 pad.4.refs_4_
  5.0 1.0 copy.42
  6.1 1.1 reshape_squeeze.3
  7.2 0.0 copy-done.1
  7.3 1.4 pad_maximum_fusion.refs_3_
  8.7 194.0 %relay.1 = (bf16[4,256,1280]{2,1,0:T(8,128)(2,1)}, bf16[4,256,1280]{2,1,0:T(8,128)(2,1)}, bf16[9,160,640]{2,1,0:T(8,128)(2,1)}, f32[16,640]{1,0:T(8,128)}) custom-call(bf16[4,256,1280]{2,1,0:T(8,128)(2,1)} %bitcast.44, bf16[4,256,1280]{2,1,0:T(8,128)(2,1)} %bitcast.45, s32[4,256]{1,0:T(4,128)} %bitcast.43, bf16[9,160,640]{2,1,0:T(8,128)(2,1)} %pad_maximum_fusion.refs_3_, ...), custom_call_target="tpu_custom_call" | custom-call | flops 24999999488 | bytes 20000000 | tf_op jit(solution)/shard_map/relay/pallas_call | solution.py:967
  202.7 0.8 fusion
  203.5 0.7 fusion.2
  204.2 0.7 fusion.1
  204.8 1.8 convert_element_type.5
  206.6 0.1 slice_bitcast_fusion.1
  206.7 1.4 slice_bitcast_fusion
  208.2 0.6 copy.34
  208.8 1.5 broadcast_in_dim_reshape.7
  210.4 0.6 copy.33
  211.0 1.5 broadcast_in_dim_reshape.6
  212.5 0.0 copy-start
  212.5 3.5 %copy.47 = bf16[1,4,1,256,1280]{4,3,2,1,0:T(8,128)(2,1)} copy(bf16[1,4,1,256,1280]{4,3,2,1,0:T(8,128)(2,1)} %bitcast.38) | data formatting | bytes 5242880
  216.1 0.0 copy-done
  216.1 1.5 copy.48
  (2 shorter events, 0.1 us)
Async XLA Ops:
  0.6 6.6 %copy-start.1 = (bf16[1,5,640,160]{2,3,1,0:T(8,128)(2,1)S(1)}, bf16[1,5,640,160]{2,3,1,0:T(8,128)(2,1)}, u32[]{:S(2)}) copy-start(bf16[1,5,640,160]{2,3,1,0:T(8,128)(2,1)} %param.20) | copy-start | bytes 3072004
  212.5 3.6 %copy-start = (bf16[4,256,1280]{2,1,0:T(8,128)(2,1)S(1)}, bf16[4,256,1280]{2,1,0:T(8,128)(2,1)}, u32[]{:S(2)}) copy-start(bf16[4,256,1280]{2,1,0:T(8,128)(2,1)} %get-tuple-element.19) | copy-start | bytes 7864324
where the time goes:
time: 219 us; the launch traced here: 218 us
  Pallas kernels  194 us (89%)
  local copies, waits for them, and re-layouts  19.7 us (9%)
  other arithmetic  3.23 us (1%)
    pallas_call x1, Pallas kernels, relay(): pl.pallas_call(functools.partial(relay_kernel, fused), out_shape=outs, in...  194 us
    unnamed x7, local copies, waits for them, and re-layouts  6.33 us

commit v1 on v0

--- a/solution.py
+++ b/solution.py
@@ -25,8 +25,10 @@
 BLOCKS = 9
 TILE = 256
 WIDE = 128
-X_STEP = 10
-A_STEP = 8
+Y_LAG, C_LAG = 1, 6
+X_STEP = 9
+F_STEP = 2
+A_STEP = C_LAG + 1
 LEAD = 3
 NN = (((1,), (0,)), ((), ()))
 NT = (((1,), (1,)), ((), ()))
@@ -35,20 +37,20 @@
 E_AT, SX_AT, LV_AT, POOL_ROWS = 0, 2 * ROWS, 4 * ROWS, 6 * ROWS
 KEEP_SLOTS, GIVE_SLOTS = 3, 3
 SCHEDULE = (
+    ("two", 6, False),
     ("compute", 0, None),
+    ("settle", 12, True),
     ("core", 1, None),
-    ("y", 3, False),
-    ("one", 3, False),
+    ("end", 8, True),
+    ("settle", 12, False),
+    ("two", 3, True),
     ("one", 1, True),
-    ("two", 5, False),
-    ("two", 3, True),
     ("end", 8, False),
-    ("end", 5, True),
-    ("settle", 11, False),
-    ("settle", 8, True),
-    ("finish", 13, None),
+    ("y", 4, False),
+    ("one", 4, False),
 )
-LAST_LAG = 13
+LAST_LAG = 12
+LATE = 2
 
 
 def dot(a, b, dims):
@@ -92,17 +94,17 @@
 
 def relay_kernel(fused, *refs):
     if fused:
-        (xin, cot, mask, wsh, vsh, bo, ig, gout, vout) = refs[:9]
-        rest = refs[9:]
+        (xin, cot, mask, w_in, w_mid, w_out) = refs[:6]
+        narrow_in, wide_in = refs[6:12], refs[12:15]
+        (bo, ig, gout, vout) = refs[15:19]
+        rest = refs[19:]
     else:
         (xin, cot, mask, wfull, wother, v640_in, v1280_in, vx_in, bo, ig, gout, vout) = refs[:12]
         rest = refs[12:]
     (W, WX, POOL, A1, S1, A2, S2, N2, A3, S3, N3, U, GM, GH, XR, ST, TG, V640, V1280, VX, AC, VS) = rest[:22]
-    (l_in, l_w, o_bo, o_ig, x_s, x_r, ha_s, ha_r, hg_s, hg_r) = rest[22:32]
+    (l_in, l_w, o_s, x_s, x_r, ha_s, ha_r, hg_s, hg_r) = rest[22:31]
     if fused:
-        (VG, CR, KEEP, GIVE, YR, ZR, YX, VR, vg_s, vg_r, gz_s, gz_r, gy_s, gy_r, gc_s, gc_r, wx_s, wx_r, wc_s, wc_r, rc_s, rc_r, ry_s, ry_r, rz_s, rz_r, fy_s, fy_r, fc_s, fc_r, vr_s, vr_r, o_g) = rest[32:]
-    else:
-        (o_g,) = rest[32:]
+        (VF, VG, CR, KEEP, GIVE, YR, ZR, YX, VR, g_s, vg_r, ga_r, gc_r, wx_r, wc_r, r_s, rc_s, rc_r, ry_r, rz_r, yx_s, fy_r, fc_r, vr_s, vr_r) = rest[31:]
 
     sec = lax.axis_index("section")
     seq = lax.axis_index("seq")
@@ -120,30 +122,45 @@
     def remote(src, dst, send, recv, where):
         return pltpu.make_async_remote_copy(src_ref=src, dst_ref=dst, send_sem=send, recv_sem=recv, device_id=where, device_id_type=MESH)
 
+    def left(send, count, width=None):
+        lines = VG.at[pl.ds(0, count)] if width else POOL.at[pl.ds(0, count), :]
+        remote(lines, lines, send, x_r.at[0], at_x).wait_send()
+
     def rows(base, m, r=0, n=LEN):
         return pl.ds(pl.multiple_of(base + m * LEN + r, 16), n)
 
-    def load_in(m, h, ref, into):
-        return pltpu.make_async_copy(ref.at[m, :, pl.ds(h * H, H)], into, l_in.at[m, h, 0 if ref is xin else 1])
-
-    for m in range(MICRO):
-        for h in range(2):
-            load_in(m, h, xin, POOL.at[pl.ds(E_AT + h * ROWS + m * LEN, LEN), :]).start()
-            load_in(m, h, cot, U.at[h, pl.ds(m * LEN, LEN), :]).start()
+    def load_in(m, h, ref, into, sem):
+        pltpu.make_async_copy(ref.at[m, 0, :, pl.ds(h * H, H)], into, sem).start()
+
+    def loaded(into, sem):
+        pltpu.make_async_copy(into, into, sem).wait()
+
     if fused:
-        own_w = pltpu.make_async_copy(wsh, W.at[:, pl.ds(pl.multiple_of(ten * PART, 16), PART), :], l_w.at[0])
-        own_v = pltpu.make_async_copy(vsh, VG.at[sec, ten], l_w.at[1])
-        own_w.start()
-        own_v.start()
+        own_rows = pl.ds(pl.multiple_of(ten * PART, 16), PART)
+        own = [pltpu.make_async_copy(w_in.at[:, pl.ds(h * H, H)], W.at[h, own_rows, :], l_w.at[h]) for h in range(2)]
+        own += [pltpu.make_async_copy(w_out.at[:, pl.ds(h * H, H)], W.at[2 + h, own_rows, :], l_w.at[2 + h]) for h in range(2)]
+        own += [pltpu.make_async_copy(w_mid, W.at[pl.ds(4, 5), own_rows, :], l_w.at[4])]
         partners = [at_core, at_y, at_diag]
         others = [(s, d) for s in range(2) for d in range(SHARDS) if s or d]
         partners += [(lax.rem(sec + s, 2), seq, lax.rem(ten + d, SHARDS)) for s, d in others]
     else:
-        own_w = pltpu.make_async_copy(wfull, W, l_w.at[0])
-        own_v = pltpu.make_async_copy(wother, WX, l_w.at[1])
-        own_w.start()
-        own_v.start()
+        own = [pltpu.make_async_copy(wfull, W, l_w.at[0]), pltpu.make_async_copy(wother, WX, l_w.at[1])]
         partners = [at_core, at_diag, at_x]
+    for copy in own:
+        copy.start()
+    for m in range(MICRO):
+        for h in range(2):
+            load_in(m, h, xin, POOL.at[pl.ds(E_AT + h * ROWS + m * LEN, LEN), :], l_in.at[0])
+            load_in(m, h, cot, U.at[h, pl.ds(m * LEN, LEN), :], l_in.at[1])
+
+    if fused:
+        VF[...] = jnp.zeros_like(VF)
+        for i, ref in enumerate(narrow_in):
+            VF[i : i + 1, 0:PART] = ref[...].astype(f32)
+        for i, ref in enumerate(wide_in):
+            for half in range(2):
+                VF[6 + 3 * half + i : 7 + 3 * half + i, 0:PART] = ref[:, half * PART : (half + 1) * PART].astype(f32)
+        VG[sec * SHARDS + ten] = VF[...].astype(bf16)
 
     barrier = pltpu.get_barrier_semaphore()
     for partner in partners:
@@ -153,50 +170,65 @@
     def piece(ref, b, s, half):
         return ref.at[b, pl.ds(pl.multiple_of(s * PART + half * HALF, 16), HALF), :]
 
-    def gz(b, s, to_up, src=None):
+    UP, DOWN, Y_, CORE_, X_, XC_, V_ = range(7)
+
+    def gz(b, s, to_up):
         spot = piece(W, b, s, core)
-        return remote(spot if src is None else src, spot, gz_s.at[b, s, 0 if to_up else 1], gz_r.at[b, s], up if to_up else down)
+        return remote(spot, spot, g_s.at[UP if to_up else DOWN], ga_r.at[b, s], up if to_up else down)
 
     def gy(b, s):
         spot = piece(W, b, s, core)
-        return remote(spot, spot, gy_s.at[b, s], gy_r.at[b, s], at_y)
-
-    def gc(b, s, half):
-        spot = piece(W, b, s, half)
-        return remote(spot, spot, gc_s.at[b, s], gc_r.at[b, s], at_core)
+        return remote(spot, spot, g_s.at[Y_], ga_r.at[b, s], at_y)
+
+    def gc(b, s):
+        spot = piece(W, b, s, core)
+        return remote(spot, spot, g_s.at[CORE_], gc_r.at[b], at_core)
+
+    def gc_here(b):
+        lines = W.at[b, pl.ds(0, (SHARDS - 1) * HALF), :]
+        remote(lines, lines, g_s.at[CORE_], gc_r.at[b], at_core).wait_recv()
 
     def wanted(b):
-        return b // 2 == sec
-
-    def gx(b, s, src=None):
+        return b // 2 == 1 - sec
+
+    def gx(b, s):
         k = lax.rem(b, 2)
-        return remote(piece(W, b, s, core) if src is None else src, piece(WX, k, s, core), wx_s.at[k, s], wx_r.at[k, s], at_x)
-
-    def gxc(k, s, half):
-        spot = piece(WX, k, s, half)
-        return remote(spot, spot, wc_s.at[k, s], wc_r.at[k, s], at_core)
+        return remote(piece(W, b, s, core), piece(WX, k, s, core), g_s.at[X_], wx_r.at[k], at_x)
+
+    def gx_here(k):
+        lines = WX.at[k, pl.ds(0, SHARDS * HALF), :]
+        remote(lines, lines, g_s.at[X_], wx_r.at[k], at_x).wait_recv()
+
+    def gxc(k, s):
+        spot = piece(WX, k, s, core)
+        return remote(spot, spot, g_s.at[XC_], wc_r.at[0], at_core)
+
+    def gv(i):
+        s, d = others[i]
+        return remote(VG.at[sec * SHARDS + ten], VG.at[sec * SHARDS + ten], g_s.at[V_], vg_r.at[0], (lax.rem(sec + s, 2), seq, lax.rem(ten + d, SHARDS)))
 
     mine = lambda b: jnp.logical_or(b == BLOCKS - 1, lax.rem(b, 2) == y)
     def send_own(b):
-        src = wsh.at[b, pl.ds(pl.multiple_of(core * HALF, 16), HALF), :]
-
         @pl.when(jnp.logical_and(mine(b), ten < SHARDS - 1))
         def _():
-            gz(b, ten, True, src).start()
+            gz(b, ten, True).start()
 
         @pl.when(jnp.logical_and(mine(b), ten > 0))
         def _():
-            gz(b, ten, False, src).start()
+            gz(b, ten, False).start()
 
         @pl.when(wanted(b))
         def _():
-            gx(b, ten, src).start()
+            gx(b, ten).start()
 
     def gather_begin():
-        for i, (s, d) in enumerate(others):
-            remote(vsh, VG.at[sec, ten], vg_s.at[i], vg_r.at[i], (lax.rem(sec + s, 2), seq, lax.rem(ten + d, SHARDS))).start()
         for b in range(LEAD):
+            own[b].wait()
             send_own(b)
+        for i in range(len(others)):
+            gv(i).start()
+        for copy in own[LEAD:]:
+            copy.wait()
 
     def gather_step(k):
         @pl.when(k + LEAD < BLOCKS)
@@ -223,14 +255,14 @@
                     def _():
                         gy(b, s).start()
 
-                    gc(b, s, core).start()
+                    gc(b, s).start()
 
                     @pl.when(wanted(b))
                     def _():
                         gx(b, s).start()
 
         for d in range(1, SHARDS):
-            b = k - d
+            b = k - d - Y_LAG
             ok = jnp.logical_and(b >= 0, b < BLOCKS)
             for above in (False, True):
                 s = ten + d if above else ten - d
@@ -239,60 +271,46 @@
                 @pl.when(jnp.logical_and(there, jnp.logical_not(mine(b))))
                 def _():
                     gy(b, s).wait_recv()
-                    gc(b, s, core).start()
+                    gc(b, s).start()
 
                     @pl.when(wanted(b))
                     def _():
                         gx(b, s).start()
 
-        b = k - 4
-        for s in range(SHARDS):
-
-            @pl.when(jnp.logical_and(jnp.logical_and(b >= 0, b < BLOCKS), s != ten))
-            def _():
-                gc(b, s, 1 - core).wait_recv()
+        b = k - C_LAG
+
+        @pl.when(jnp.logical_and(b >= 0, b < BLOCKS))
+        def _():
+            gc_here(b)
 
         @pl.when(jnp.logical_and(k >= X_STEP, k < X_STEP + 2))
         def _():
+            gx_here(k - X_STEP)
             for s in range(SHARDS):
-                gx(k - X_STEP, s).wait_recv()
-                gxc(k - X_STEP, s, core).start()
+                gxc(k - X_STEP, s).start()
 
     def others_blocks():
-        for k in range(2):
-            for s in range(SHARDS):
-                gxc(k, s, 1 - core).wait_recv()
-
-    def gather_drain(b):
-        @pl.when(b < 2)
-        def _():
-            for s in range(SHARDS):
-                gx(b, s).wait_send()
-                gxc(b, s, core).wait_send()
-
-        for s in range(SHARDS):
-            fromabove = s > ten
-
-            @pl.when(jnp.logical_and(mine(b), jnp.logical_and(s <= ten, ten < SHARDS - 1)))
-            def _():
-                gz(b, s, True).wait_send()
-
-            @pl.when(jnp.logical_and(mine(b), jnp.logical_and(s >= ten, ten > 0)))
-            def _():
-                gz(b, s, False).wait_send()
-
-            @pl.when(s != ten)
-            def _():
-                gc(b, s, core).wait_send()
-
-                @pl.when(jnp.logical_and(mine(b), b < BLOCKS - 1))
-                def _():
-                    gy(b, s).wait_send()
+        lines = POOL.at[pl.ds(0, 2 * SHARDS * HALF), :]
+        remote(lines, lines, g_s.at[XC_], wc_r.at[0], at_core).wait_recv()
+
+    def gather_drain():
+        left(g_s.at[V_], len(others), True)
+        left(g_s.at[Y_], 4 * (SHARDS - 1) * HALF)
+        left(g_s.at[CORE_], BLOCKS * (SHARDS - 1) * HALF)
+        left(g_s.at[X_], 2 * SHARDS * HALF)
+        left(g_s.at[XC_], 2 * SHARDS * HALF)
+        for z in range(SHARDS):
+
+            @pl.when(ten == z)
+            def _():
+                if z < SHARDS - 1:
+                    left(g_s.at[UP], 5 * (z + 1) * HALF)
+                if z > 0:
+                    left(g_s.at[DOWN], 5 * (SHARDS - z) * HALF)
 
     def vectors():
-        own_v.wait()
-        for i, (s, d) in enumerate(others):
-            remote(vsh, VG.at[sec, ten], vg_s.at[i], vg_r.at[i], at_x).wait()
+        lines = VG.at[pl.ds(0, len(others))]
+        remote(lines, lines, g_s.at[V_], vg_r.at[0], at_x).wait_recv()
         line = lax.broadcasted_iota(jnp.int32, (2 * 128, H), 0)
         col = lax.broadcasted_iota(jnp.int32, (2 * 128, H), 1)
 
@@ -303,9 +321,9 @@
         wide = [[jnp.zeros((16, H), f32) for _ in range(4)] for _ in range(2)]
         for s in range(SHARDS):
             inner = pick(s * PART)
-            narrow = narrow + dot(VG[sec, s], inner, NN)
+            narrow = narrow + dot(VG[sec * SHARDS + s], inner, NN)
             for who in range(2):
-                held = VG[sec if who == 0 else 1 - sec, s]
+                held = VG[(sec if who == 0 else 1 - sec) * SHARDS + s]
                 for h in range(2):
                     for k in range(2):
                         put = pick(s * 2 * PART + k * PART - h * H)
@@ -316,29 +334,30 @@
                 into[h, 0:3, :] = wide[who][h * 2][6:9] + wide[who][h * 2 + 1][9:12]
 
     def halo(ref, sends, recvs, m, reach, start):
-        fwd = remote(ref.at[m, pl.ds(2 * LEN - reach, reach), :], ref.at[m, pl.ds(LEN - reach, reach), :], sends.at[m, 0], recvs.at[m, 0], ahead)
-        bwd = remote(ref.at[m, pl.ds(LEN, reach), :], ref.at[m, pl.ds(2 * LEN, reach), :], sends.at[m, 1], recvs.at[m, 1], behind)
+        fwd = remote(ref.at[m, pl.ds(2 * LEN - reach, reach), :], ref.at[m, pl.ds(LEN - reach, reach), :], sends.at[0], recvs.at[m, 0], ahead)
+        bwd = remote(ref.at[m, pl.ds(LEN, reach), :], ref.at[m, pl.ds(2 * LEN, reach), :], sends.at[1], recvs.at[m, 1], behind)
 
         @pl.when(seq < 3)
         def _():
-            fwd.start() if start else fwd.wait_send()
+            fwd.start() if start else bwd.wait_recv()
 
         @pl.when(seq > 0)
         def _():
-            bwd.start() if start else bwd.wait_send()
-
-        if not start:
-
-            @pl.when(seq > 0)
-            def _():
-                fwd.wait_recv()
-
-            @pl.when(seq < 3)
-            def _():
-                bwd.wait_recv()
+            bwd.start() if start else fwd.wait_recv()
+
+    def halo_drain(sends):
+        for s, reach in ((0, 2 * SPAN_0), (1, 2 * SPAN_1)):
+
+            @pl.when(jnp.logical_and(sec == s, seq < 3))
+            def _():
+                left(sends.at[0], MICRO * reach)
+
+            @pl.when(jnp.logical_and(sec == s, seq > 0))
+            def _():
+                left(sends.at[1], MICRO * reach)
 
     def x_send(m, src):
-        return remote(src.at[rows(0, m), :], XR.at[rows(0, m), :], x_s.at[m], x_r.at[m], at_x)
+        return remote(src.at[rows(0, m), :], XR.at[rows(0, m), :], x_s.at[0], x_r.at[m], at_x)
 
     def stage_first(m):
         def tile(i):
@@ -358,7 +377,7 @@
 
     def stage_a(m, reach):
         here = rows(0, m)
-        TG[0:LEN, :] = dot(A1[0, here, :], W[2], NT) + dot(A1[1, here, :], W[3], NT)
+        TG[0:LEN, :] = dot(A1[0, here, :], W[0], NT) + dot(A1[1, here, :], W[1], NT)
 
         def tile2(i):
             r = i * TILE
@@ -398,15 +417,15 @@
             x_send(m, A3).start()
         here = rows(0, m)
         for h in range(2):
-            mixed = dot(A3[here, :], W[h], NN) + V1280[h, 0:1, :]
+            mixed = dot(A3[here, :], W[2 + h], NN) + V1280[h, 0:1, :]
             POOL[rows(LV_AT + h * ROWS, m), :] = (POOL[rows(E_AT + h * ROWS, m), :].astype(f32) + mixed).astype(bf16)
             out_bo(m, h).start()
 
     def out_bo(m, h):
-        return pltpu.make_async_copy(POOL.at[rows(LV_AT + h * ROWS, m), :], bo.at[m, :, pl.ds(h * H, H)], o_bo.at[m, h])
+        return pltpu.make_async_copy(POOL.at[rows(LV_AT + h * ROWS, m), :], bo.at[m, :, pl.ds(h * H, H)], o_s.at[0])
 
     def out_ig(m, h):
-        return pltpu.make_async_copy(S1.at[h, rows(0, m), :], ig.at[m, :, pl.ds(h * H, H)], o_ig.at[m, h])
+        return pltpu.make_async_copy(S1.at[h, rows(0, m), :], ig.at[m, :, pl.ds(h * H, H)], o_s.at[1])
 
     def stage_x(m):
         x_send(m, A3).wait_recv()
@@ -451,7 +470,7 @@
 
     def back_three(m):
         here = rows(0, m)
-        TG[LEN : 2 * LEN, :] = dot(U[0, here, :], W[0], NT) + dot(U[1, here, :], W[1], NT)
+        TG[LEN : 2 * LEN, :] = dot(U[0, here, :], W[2], NT) + dot(U[1, here, :], W[3], NT)
 
     def stage_p1(m, reach):
         back_three(m)
@@ -495,7 +514,7 @@
 
     def stage_p3(m):
         for h in range(2):
-            TG[h * LEN : (h + 1) * LEN, :] = dot(GH[rows(0, m), :], W[2 + h], NN)
+            TG[h * LEN : (h + 1) * LEN, :] = dot(GH[rows(0, m), :], W[h], NN)
 
         def tile(i):
             r = i * WIDE
@@ -530,11 +549,9 @@
                     ref[m, 2 * LEN : 3 * LEN, :] = jnp.zeros((LEN, H), bf16)
 
         for m in range(MICRO):
-            ST[m * LEN : (m + 1) * LEN, 6:7] = jnp.transpose(jnp.broadcast_to(mask[m : m + 1, :].astype(f32), (128, LEN)))[:, 0:1]
-        for m in range(MICRO):
-            for h in range(2):
-                load_in(m, h, xin, POOL.at[pl.ds(E_AT + h * ROWS + m * LEN, LEN), :]).wait()
-                load_in(m, h, cot, U.at[h, pl.ds(m * LEN, LEN), :]).wait()
+            ST[m * LEN : (m + 1) * LEN, 6:7] = jnp.transpose(jnp.broadcast_to(mask[m].astype(f32), (128, LEN)))[:, 0:1]
+        loaded(POOL.at[pl.ds(E_AT, 2 * ROWS), :], l_in.at[0])
+        loaded(U, l_in.at[1])
 
         def masked(m):
             at = rows(0, m)
@@ -550,25 +567,27 @@
     if fused:
         gather_begin()
         prepare()
-        own_w.wait()
-        vectors()
         early = MICRO
 
         def step(k):
             gather_step(k)
 
-            @pl.when(jnp.logical_and(first, jnp.logical_and(k >= 1, k < 1 + MICRO)))
-            def _():
-                stage_first(k - 1)
+            @pl.when(k == F_STEP)
+            def _():
+                vectors()
+
+            @pl.when(jnp.logical_and(first, jnp.logical_and(k >= F_STEP, k < F_STEP + MICRO)))
+            def _():
+                stage_first(k - F_STEP)
 
             @pl.when(jnp.logical_and(first, jnp.logical_and(k >= A_STEP, k < A_STEP + MICRO)))
             def _():
                 stage_a(k - A_STEP, 2 * SPAN_0)
 
-        loop(BLOCKS + 4, step)
+        loop(BLOCKS + C_LAG, step)
     else:
-        own_w.wait()
-        own_v.wait()
+        for copy in own:
+            copy.wait()
         for src, dst in ((v640_in, V640), (v1280_in, V1280), (vx_in, VX)):
             dst[...] = src[...]
         prepare()
@@ -590,13 +609,10 @@
             stage_q(m)
             stage_p1(m, 2 * SPAN_0)
 
-            @pl.when(m > 0)
-            def _():
+            @pl.when(jnp.logical_and(m > 0, m < MICRO - 1))
+            def _():
+                stage_p2(m - 1, SPAN_0, False)
                 stage_p3(m - 1)
-
-            @pl.when(m < MICRO - 1)
-            def _():
-                stage_p2(m, SPAN_0, False)
 
         loop(MICRO, backward)
 
@@ -606,61 +622,53 @@
             others_blocks()
 
         def both(k):
-            @pl.when(k == MICRO + 1)
-            def _():
-                loop(MICRO - 1, stage_p3)
-
             @pl.when(k < MICRO)
             def _():
                 stage_x(k)
                 stage_first(k)
                 stage_a(k, 2 * SPAN_1)
 
-            inner = jnp.logical_and(k >= 1, k <= MICRO)
-
-            @pl.when(inner)
+            @pl.when(jnp.logical_and(k >= 1, k <= MICRO))
             def _():
                 stage_b(k - 1, SPAN_1, False)
+                stage_p1(k - 1, 2 * SPAN_1)
+
+            @pl.when(k == MICRO + 1)
+            def _():
+                loop(MICRO - LATE, stage_p3)
 
             @pl.when(k >= 2)
             def _():
                 stage_p2(k - 2, SPAN_1, True)
-
-            @pl.when(inner)
-            def _():
-                stage_p1(k - 1, 2 * SPAN_1)
 
         loop(MICRO + 2, both)
 
     def last_grad_hidden():
         @pl.when(first)
         def _():
-            stage_p2(MICRO - 1, SPAN_0, False)
-
-    def last_input_grad():
-        stage_p3(MICRO - 1)
+            loop(LATE, lambda m: stage_p2(m + MICRO - LATE, SPAN_0, False))
+
+    def small_gradients():
         for i in range(12):
             VS[0, i : i + 1, :] = jnp.sum(AC[i], axis=0, keepdims=True)
         VS[0, 12:16, :] = jnp.zeros((4, H), f32)
 
     def relay_drain():
-        loop(MICRO, lambda m: x_send(m, A3).wait_send())
-
-        def out_wait(m):
-            for h in range(2):
-                out_bo(m, h).wait()
-                out_ig(m, h).wait()
-
-        loop(MICRO, out_wait)
+        left(x_s.at[0], ROWS)
+        halo_drain(ha_s)
+        halo_drain(hg_s)
+        for i in range(2):
+            lines = POOL.at[pl.ds(0, 2 * ROWS), :]
+            pltpu.make_async_copy(lines, lines, o_s.at[i]).wait()
 
     def gradient(b):
         @pl.when(b < 2)
         def _():
-            TG[...] = dot(A3[...], U[b], TN)
+            TG[...] = dot(GH[...], A1[b], TN)
 
         @pl.when(jnp.logical_and(b >= 2, b < 4))
         def _():
-            TG[...] = dot(GH[...], A1[b - 2], TN)
+            TG[...] = dot(A3[...], U[b - 2], TN)
 
         @pl.when(b >= 4)
         def _():
@@ -669,12 +677,13 @@
 
     if not fused:
         last_grad_hidden()
-        last_input_grad()
+        loop(LATE, lambda m: stage_p3(m + MICRO - LATE))
+        small_gradients()
         relay_drain()
 
         def whole(b):
             gradient(b)
-            out = pltpu.make_async_copy(TG, gout.at[b], o_g.at[b])
+            out = pltpu.make_async_copy(TG, gout.at[b], l_w.at[0])
             out.start()
             out.wait()
 
@@ -687,7 +696,7 @@
     over_tensor_first = lambda p: kind(p) == 2
     zslot = lambda p: slot(p) + jnp.where(over_tensor_first(p), 3, 0)
     owned = lambda p: jnp.logical_or(over_tensor_first(p), kind(p) == y)
-    block = lambda p: jnp.where(p < 2, p, jnp.where(p < 7, p + 2, p - 5))
+    block = lambda p: jnp.where(p < 7, p + 2, p - 7)
     outer = jnp.logical_or(ten == 0, ten == SHARDS - 1)
     low_side = ten < SHARDS // 2
     FAR, NEAR = jnp.where(low_side, 3, 0), jnp.where(low_side, 2, 1)
@@ -705,22 +714,27 @@
         return gout.at[block(p), half_of(half), :]
 
     def rc(p):
-        return remote(GIVE.at[lax.rem(p, GIVE_SLOTS)], CR.at[p], rc_s.at[p], rc_r.at[p], at_core)
-
-    def ry(p, s):
-        return remote(part(p, s), YR.at[slot(p), s], ry_s.at[slot(p), s], ry_r.at[slot(p), s], at_y)
-
-    def rz(p, s, idx_send, idx, to):
-        return remote(part(p, s), ZR.at[zslot(p), idx], rz_s.at[zslot(p), idx_send], rz_r.at[zslot(p), idx], (sec, seq, to))
-
-    def fy(p, into):
-        return remote(part(p, ten), into, fy_s.at[p], fy_r.at[p], at_y)
-
-    def fc(p, src, half):
-        return remote(src, final(p, half), fc_s.at[p], fc_r.at[p], at_core)
+        return remote(GIVE.at[lax.rem(p, GIVE_SLOTS)], CR.at[p], rc_s.at[lax.rem(p, GIVE_SLOTS)], rc_r.at[p], at_core)
+
+    R_Y, R_Z, R_FY, R_FC, R_OUT = range(5)
+
+    def ry(p):
+        return remote(CR.at[p], YR.at[slot(p)], r_s.at[R_Y], ry_r.at[slot(p)], at_y)
+
+    def rz(p, s, idx, to):
+        return remote(part(p, s), ZR.at[zslot(p), idx], r_s.at[R_Z], rz_r.at[zslot(p), idx], (sec, seq, to))
+
+    def yx(p):
+        return remote(part(p, ten), YX.at[slot(p)], yx_s.at[slot(p)], fy_r.at[p], at_y)
+
+    def fy(p):
+        return remote(part(p, ten), final(p, core), r_s.at[R_FY], fy_r.at[p], at_y)
+
+    def fc(p, src):
+        return remote(src, final(p, core), r_s.at[R_FC], fc_r.at[0], at_core)
 
     def out_g(p):
-        return pltpu.make_async_copy(part(p, ten), final(p, core), o_g.at[p])
+        return pltpu.make_async_copy(part(p, ten), final(p, core), r_s.at[R_OUT])
 
     def add(ref, *others_):
         total = ref[...].astype(f32)
@@ -743,19 +757,19 @@
 
     def over_core(p):
         rc(p).wait_recv()
-        for s in (0, 3, 1, 2):
+        for s in range(SHARDS):
             add(part(p, s), kept(p, s))
 
-            @pl.when(jnp.logical_not(owned(p)))
-            def _():
-                ry(p, s).start()
+        @pl.when(jnp.logical_not(owned(p)))
+        def _():
+            ry(p).start()
 
     def over_y(p):
         @pl.when(owned(p))
         def _():
-            for s in (0, 3, 1, 2):
-                ry(p, s).wait_recv()
-                add(part(p, s), YR.at[slot(p), s])
+            ry(p).wait_recv()
+            for s in range(SHARDS):
+                add(part(p, s), YR.at[slot(p), s * HALF : (s + 1) * HALF, :])
 
     def chain_one(p):
         @pl.when(jnp.logical_and(owned(p), outer))
@@ -763,54 +777,51 @@
             for k in range(3):
                 s = jnp.where(low_side, 3 - k, k)
                 idx = jnp.where(low_side, s - 1, s)
-                rz(p, s, idx, idx, jnp.where(low_side, 1, 2)).start()
+                rz(p, s, idx, jnp.where(low_side, 1, 2)).start()
 
         @pl.when(jnp.logical_and(owned(p), jnp.logical_not(outer)))
         def _():
             s = jnp.where(low_side, 0, 3)
-            rz(p, s, 0, 0, s).start()
+            rz(p, s, 0, s).start()
 
     def chain_two(p):
         @pl.when(jnp.logical_and(owned(p), jnp.logical_not(outer)))
         def _():
-            for s, idx, idx_send in ((FAR, jnp.where(low_side, 2, 0), 1), (NEAR, 1, 2)):
-                rz(p, s, idx_send, idx, s).wait_recv()
+            for s, idx in ((FAR, jnp.where(low_side, 2, 0)), (NEAR, 1)):
+                rz(p, s, idx, s).wait_recv()
                 add(part(p, s), ZR.at[zslot(p), idx])
-                rz(p, s, idx_send, 3, s).start()
+                rz(p, s, 3, s).start()
 
     def chain_end(p):
         @pl.when(owned(p))
         def _():
-            idx = jnp.where(ten == 2, 2, 0)
-            rz(p, ten, 0, idx, ten).wait_recv()
-            rz(p, ten, 0, 3, ten).wait_recv()
+            idx, at_z = jnp.where(ten == 2, 2, 0), lax.rem(ten + 1, SHARDS)
+            rz(p, ten, idx, at_z).wait_recv()
+            rz(p, ten, 3, at_z).wait_recv()
             add(part(p, ten), ZR.at[zslot(p), idx], ZR.at[zslot(p), 3])
 
             @pl.when(over_tensor_first(p))
             def _():
-                fy(p, YX.at[slot(p)]).start()
+                yx(p).start()
 
             @pl.when(jnp.logical_not(over_tensor_first(p)))
             def _():
-                fy(p, final(p, core)).start()
-                fc(p, part(p, ten), core).start()
+                fy(p).start()
+                fc(p, part(p, ten)).start()
                 out_g(p).start()
 
     def settle(p):
         @pl.when(over_tensor_first(p))
         def _():
-            fy(p, YX.at[slot(p)]).wait()
+            yx(p).wait()
             add(part(p, ten), YX.at[slot(p)])
-            fc(p, part(p, ten), core).start()
+            fc(p, part(p, ten)).start()
             out_g(p).start()
 
         @pl.when(jnp.logical_not(owned(p)))
         def _():
-            fy(p, final(p, core)).wait_recv()
-            fc(p, final(p, core), core).start()
-
-    def finish(p):
-        fc(p, part(p, ten), 1 - core).wait_recv()
+            fy(p).wait_recv()
+            fc(p, final(p, core)).start()
 
     def vector_round(i):
         pair, far = ten + 1 - 2 * lax.rem(ten, 2), lax.rem(ten + 2, SHARDS)
@@ -819,26 +830,31 @@
         return remote(VS.at[i], VR.at[i], vr_s.at[i], vr_r.at[i], (sec, where_seq, where_ten))
 
     def sums(t):
+        @pl.when(t == BLOCKS - 2)
+        def _():
+            last_grad_hidden()
+
         for stage, lag, first_kind in SCHEDULE:
             p = t - lag
             fits = jnp.logical_and(p >= 0, p < BLOCKS)
             if first_kind is not None:
                 fits = jnp.logical_and(fits, over_tensor_first(p) if first_kind else jnp.logical_not(over_tensor_first(p)))
-            if stage == "compute":
-
-                @pl.when(p == BLOCKS - 2)
-                def _():
-                    last_grad_hidden()
 
             @pl.when(fits)
             def _():
-                dict(compute=compute, core=over_core, y=over_y, one=chain_one, two=chain_two, end=chain_end, settle=settle, finish=finish)[stage](p)
-
-        @pl.when(t == BLOCKS)
-        def _():
-            last_input_grad()
-
-        i = t - BLOCKS - 1
+                dict(compute=compute, core=over_core, y=over_y, one=chain_one, two=chain_two, end=chain_end, settle=settle)[stage](p)
+
+        late = t - BLOCKS
+
+        @pl.when(jnp.logical_and(late >= 0, late < LATE))
+        def _():
+            stage_p3(late + MICRO - LATE)
+
+        i = late - LATE
+
+        @pl.when(i == 0)
+        def _():
+            small_gradients()
 
         @pl.when(jnp.logical_and(i > 0, i <= 4))
         def _():
@@ -852,33 +868,16 @@
     loop(BLOCKS + LAST_LAG, sums)
     vout[...] = VS[4]
 
+    lines = POOL.at[pl.ds(0, BLOCKS * HALF), :]
+    remote(lines, lines, r_s.at[R_FC], fc_r.at[0], at_core).wait()
     relay_drain()
-    loop(BLOCKS, gather_drain)
-
-    def drain(p):
-        @pl.when(p >= BLOCKS - GIVE_SLOTS)
-        def _():
-            rc(p).wait_send()
-
-        fc(p, part(p, ten), core).wait_send()
-
-        @pl.when(owned(p))
-        def _():
-            out_g(p).wait()
-
-            @pl.when(jnp.logical_not(over_tensor_first(p)))
-            def _():
-                fy(p, final(p, core)).wait_send()
-
-            for k in range(3):
-                rz(p, ten, k, 0, ten).wait_send()
-
-        @pl.when(jnp.logical_not(owned(p)))
-        def _():
-            for s in range(SHARDS):
-                ry(p, s).wait_send()
-
-    loop(BLOCKS, drain)
+    gather_drain()
+    loop(GIVE_SLOTS, lambda i: rc(i).wait_send())
+    left(r_s.at[R_Y], 3 * SHARDS * HALF)
+    left(r_s.at[R_Z], 6 * 3 * HALF)
+    left(r_s.at[R_FY], 3 * HALF)
+    lines = POOL.at[pl.ds(0, 6 * HALF), :]
+    pltpu.make_async_copy(lines, lines, r_s.at[R_OUT]).wait()
 
 
 def relay(block_input, cotangent, mask, weights, vectors, fused):
@@ -910,60 +909,51 @@
         full(2, 8, H),
         full(12, 8, H),
         full(5, 16, H),
-        dma(MICRO, 2, 2),
+        dma(2),
+        dma(5),
+        dma(2),
+        dma(1),
+        dma(MICRO),
         dma(2),
         dma(MICRO, 2),
-        dma(MICRO, 2),
-        dma(MICRO),
-        dma(MICRO),
-        dma(MICRO, 2),
-        dma(MICRO, 2),
-        dma(MICRO, 2),
+        dma(2),
         dma(MICRO, 2),
     ]
     if fused:
         scratch += [
-            low(2, SHARDS, 16, 256),
+            full(16, 256),
+            low(2 * SHARDS, 16, 256),
             low(BLOCKS, SHARDS * HALF, H),
             low(KEEP_SLOTS, SHARDS * HALF, H),
             low(GIVE_SLOTS, SHARDS * HALF, H),
-            low(3, SHARDS, HALF, H),
+            low(3, SHARDS * HALF, H),
             low(6, 4, HALF, H),
             low(3, HALF, H),
             full(4, 16, H),
             dma(7),
-            dma(7),
-            dma(BLOCKS, SHARDS, 2),
+            dma(1),
             dma(BLOCKS, SHARDS),
-            dma(BLOCKS, SHARDS),
-            dma(BLOCKS, SHARDS),
-            dma(BLOCKS, SHARDS),
-            dma(BLOCKS, SHARDS),
-            dma(2, SHARDS),
-            dma(2, SHARDS),
-            dma(2, SHARDS),
-            dma(2, SHARDS),
             dma(BLOCKS),
+            dma(2),
+            dma(1),
+            dma(5),
+            dma(GIVE_SLOTS),
             dma(BLOCKS),
-            dma(3, SHARDS),
-            dma(3, SHARDS),
-            dma(6, 3),
+            dma(3),
             dma(6, 4),
+            dma(3),
             dma(BLOCKS),
-            dma(BLOCKS),
-            dma(BLOCKS),
-            dma(BLOCKS),
+            dma(1),
             dma(4),
             dma(4),
         ]
-    scratch += [dma(BLOCKS)]
     outs = (
         jax.ShapeDtypeStruct((MICRO, LEN, 2 * H), bf16),
         jax.ShapeDtypeStruct((MICRO, LEN, 2 * H), bf16),
         jax.ShapeDtypeStruct((BLOCKS, PART, H), bf16) if fused else jax.ShapeDtypeStruct((BLOCKS, H, H), f32),
         jax.ShapeDtypeStruct((16, H), f32),
     )
-    in_specs = [hbm, hbm, vmem] + [hbm] * len(weights) + ([hbm] if fused else [vmem] * 3)
+    in_specs = [hbm, hbm, vmem] + [hbm] * len(weights) + [vmem] * len(vectors)
     return pl.pallas_call(
         functools.partial(relay_kernel, fused),
         out_shape=outs,
@@ -976,10 +966,75 @@
     )(block_input, cotangent, mask, *weights, *vectors)
 
 
+def unpack_kernel(bo, ig, grads, small, bo_out, ig_out, in_out, mid_out, out_out, *rest):
+    vectors, (B, G, F, sems) = rest[:9], rest[9:]
+    ten = lax.axis_index("tensor")
+    load = pltpu.make_async_copy(grads, G, sems.at[2, 0])
+    load.start()
+    arrays = [(k, m, src, dst) for k, (src, dst) in enumerate(((bo, bo_out), (ig, ig_out))) for m in range(MICRO)]
+    arrive = [pltpu.make_async_copy(src.at[m], B.at[k, m], sems.at[k, m]) for k, m, src, dst in arrays]
+    leave = [pltpu.make_async_copy(B.at[k, m], dst.at[0, m, 0], sems.at[4 + k, m]) for k, m, src, dst in arrays]
+    for copy in arrive:
+        copy.start()
+    for z in range(SHARDS):
+
+        @pl.when(ten == z)
+        def _():
+            for row, ref in zip((0, 1, 2, 3, 4, 5), vectors[:6]):
+                ref[...] = small[row : row + 1, z * PART : (z + 1) * PART]
+            for i, ref in enumerate(vectors[6:]):
+                row, at = 6 + 2 * i + z // 2, z % 2 * 2 * PART
+                ref[...] = small[row : row + 1, at : at + 2 * PART]
+
+    load.wait()
+    F[...] = G[...].astype(f32)
+    outs = [pltpu.make_async_copy(F.at[h + 2 * k], ref.at[:, pl.ds(h * H, H)], sems.at[3, 2 * k + h]) for k, ref in enumerate((in_out, out_out)) for h in range(2)]
+    outs += [pltpu.make_async_copy(F.at[pl.ds(4, 5)], mid_out, sems.at[2, 1])]
+    for out in outs:
+        out.start()
+    for came, copy in zip(arrive, leave):
+        came.wait()
+        copy.start()
+    for copy in leave + outs:
+        copy.wait()
+
+
+def unpacked(block_out, input_grad, grads, small):
+    hbm, vmem = pl.BlockSpec(memory_space=pl.ANY), pl.BlockSpec(memory_space=pltpu.VMEM)
+    like = lambda *shape: jax.ShapeDtypeStruct(shape, f32)
+    rows_like = jax.ShapeDtypeStruct((1, MICRO, 1, LEN, 2 * H), bf16)
+    (block_out, input_grad, grad_in, grad_mid, grad_out, *vectors) = pl.pallas_call(
+        unpack_kernel,
+        out_shape=[rows_like, rows_like, like(PART, 2 * H), like(5, PART, H), like(PART, 2 * H)] + [like(1, PART)] * 6 + [like(1, 2 * PART)] * 3,
+        in_specs=[hbm, hbm, hbm, vmem],
+        out_specs=[hbm] * 5 + [vmem] * 9,
+        scratch_shapes=[pltpu.VMEM((2, MICRO, LEN, 2 * H), bf16), pltpu.VMEM((BLOCKS, PART, H), bf16), pltpu.VMEM((BLOCKS, PART, H), f32), pltpu.SemaphoreType.DMA((6, MICRO))],
+        compiler_params=pltpu.CompilerParams(vmem_limit_bytes=62 * 2**20),
+        name="unpack",
+    )(block_out, input_grad, grads, small)
+    (bias_in, bias_mid, gain_second, shift_second, gain_third, shift_third, bias_out, gain_first, shift_first) = vectors
+    return (
+        block_out,
+        input_grad,
+        grad_in.T[None],
+        bias_in,
+        grad_mid.transpose(0, 2, 1)[None],
+        bias_mid,
+        grad_out[None],
+        bias_out,
+        gain_first,
+        shift_first,
+        gain_second,
+        shift_second,
+        gain_third,
+        shift_third,
+    )
+
+
 def packed_weights(conv_in, conv_mid, conv_out):
     channels = conv_out.shape[0]
     halves = lambda m: m.reshape(channels, 2, H).transpose(1, 0, 2)
-    return jnp.concatenate([halves(conv_out), halves(conv_in.T), conv_mid.transpose(0, 2, 1)])
+    return jnp.concatenate([halves(conv_in.T), halves(conv_out), conv_mid.transpose(0, 2, 1)])
 
 
 def local(*args):
@@ -989,32 +1044,28 @@
     shards = lax.axis_size("tensor")
     fused = shards == SHARDS
     channels = conv_out.shape[0]
-    xin = block_input.reshape(MICRO, LEN, 2 * H)
-    cot = cotangent.reshape(MICRO, LEN, 2 * H)
-    mask = mask.reshape(MICRO, LEN)
-    mine = packed_weights(conv_in, conv_mid, conv_out)
     narrow = (bias_in, bias_mid, gain_second, shift_second, gain_third, shift_third)
     wide = (bias_out, gain_first, shift_first)
     if fused:
-        lines = jnp.stack(list(narrow) + [w[:PART] for w in wide] + [w[PART:] for w in wide])
-        vsh = jnp.pad(lines, ((0, 4), (0, 256 - PART)))
-        block_out, input_grad, grads, small = relay(xin, cot, mask, (mine,), (vsh,), True)
-        grads = grads.astype(f32)
+        weights = (conv_in.T, conv_mid.transpose(0, 2, 1), conv_out)
+        block_out, input_grad, grads, small = relay(block_input, cotangent, mask, weights, tuple(v[None] for v in narrow + wide), True)
+        return unpacked(block_out, input_grad, grads, small)
     else:
+        mine = packed_weights(conv_in, conv_mid, conv_out)
         whole = lax.all_gather(mine, "tensor", axis=1, tiled=True)
         swap = [(0, 1), (1, 0)]
-        give = jnp.where(sec == 0, whole[0:2], whole[2:4])
+        give = jnp.where(sec == 0, whole[2:4], whole[0:2])
         other = lax.ppermute(give, "section", swap)
         v_narrow = lax.all_gather(jnp.stack(narrow), "tensor", axis=1, tiled=True)
         v_wide = lax.all_gather(jnp.stack(wide), "tensor", axis=1, tiled=True)
         v640 = jnp.pad(v_narrow.astype(f32), ((0, 10), (0, 0)))
         v1280 = jnp.pad(v_wide.astype(f32).reshape(3, 2, H).transpose(1, 0, 2), ((0, 0), (0, 5), (0, 0)))
         vx = lax.ppermute(v1280, "section", swap)
-        block_out, input_grad, grads, small = relay(xin, cot, mask, (whole, other), (v640, v1280, vx), False)
+        block_out, input_grad, grads, small = relay(block_input, cotangent, mask, (whole, other), (v640, v1280, vx), False)
         grads = lax.psum(lax.psum_scatter(grads, "tensor", scatter_dimension=1, tiled=True), "seq")
         small = lax.psum(small, ("seq", "tensor"))
-    grad_in = grads[2:4].transpose(0, 2, 1).reshape(2 * H, channels)
-    grad_out = grads[0:2].transpose(1, 0, 2).reshape(channels, 2 * H)
+    grad_in = grads[0:2].transpose(0, 2, 1).reshape(2 * H, channels)
+    grad_out = grads[2:4].transpose(1, 0, 2).reshape(channels, 2 * H)
     grad_mid = grads[4:9].transpose(0, 2, 1)
     thin = lax.dynamic_slice_in_dim(small[0:6], ten * channels, channels, 1)
     thick = lax.dynamic_slice_in_dim(small[6:12].reshape(3, 2 * H), ten * 2 * channels, 2 * channels, 1)

time: 219 us -> 185 us (0.84)
  local copies, waits for them, and re-layouts: 19.7 us -> 0 us
  Pallas kernels: 194 us -> 184 us
  other arithmetic: 3.23 us -> 0 us
    pallas_call x1, Pallas kernels: 194 us -> 178 us  [relay(): pl.pallas_call(functools.partial(relay_kernel, fused), out_shape=outs, in...]
    pallas_call x0 -> x1, Pallas kernels: none -> 6.78 us  [unpacked(): pl.pallas_call(unpack_kernel, out_shape=[rows_like, rows_like, like(PART,...]
    unnamed x7 -> x0, local copies, waits for them, and re-layouts: 6.33 us -> none
    another operation x5 -> x0, local copies, waits for them, and re-layouts: 5.05 us -> none  [the longest x1 1.55 us: local(): grad_out[None]]
    slice x5 -> x0, local copies, waits for them, and re-layouts: 3.81 us -> none  [the longest x2 1.69 us: local(): w[PART:]]
where the time goes in v1:
time: 185 us
  Pallas kernels  184 us (99%)
    pallas_call x1, Pallas kernels, relay(): pl.pallas_call(functools.partial(relay_kernel, fused), out_shape=outs, in...  178 us
    pallas_call x1, Pallas kernels, unpacked(): pl.pallas_call(unpack_kernel, out_shape=[rows_like, rows_like, like(PART,...  6.78 us

profile of v1, /device:TPU:0, one launch (start us, length us, event | category | flops | bytes accessed | tf_op | source)
XLA Modules:
  0.0 185.2 jit_solution(4582797048732124568)
XLA Ops:
  0.7 177.6 %relay.1 = (bf16[4,256,1280]{2,1,0:T(8,128)(2,1)}, bf16[4,256,1280]{2,1,0:T(8,128)(2,1)}, bf16[9,160,640]{2,1,0:T(8,128)(2,1)}, f32[16,640]{1,0:T(8,128)}) custom-call(bf16[4,1,256,1280]{3,2,1,0:T(8,128)(2,1)} %refs_0_.1, bf16[4,1,256,1280]{3,2,1,0:T(8,128)(2,1)} %refs_1_.1, s32[4,1,256]{2,1,0:T(1,128)} %refs_2_.1, bf16[160,1280]{1,0:T(8,128)(2,1)} %bitcast.18, ...), custom_call_target="tpu_custom_call" | custom-call | flops 24999999488 | bytes 20000000 | tf_op jit(solution)/shard_map/relay/pallas_call | solution.py:957
  178.2 6.8 %unpack.1 = (bf16[1,4,1,256,1280]{4,3,2,1,0:T(8,128)(2,1)}, bf16[1,4,1,256,1280]{4,3,2,1,0:T(8,128)(2,1)}, f32[160,1280]{1,0:T(8,128)}, f32[5,160,640]{2,1,0:T(8...) custom-call(bf16[4,256,1280]{2,1,0:T(8,128)(2,1)} %get-tuple-element, ...), custom_call_target="tpu_custom_call" | custom-call | tf_op jit(solution)/shard_map/unpack/pallas_call | solution.py:1006

commit v2 on v1

--- a/solution.py
+++ b/solution.py
@@ -23,6 +23,8 @@
 PART = H // SHARDS
 HALF = PART // 2
 BLOCKS = 9
+LAST = BLOCKS - 1
+GUEST, GUEST_TURN = BLOCKS, 3
 TILE = 256
 WIDE = 128
 Y_LAG, C_LAG = 1, 6
@@ -50,7 +52,7 @@
     ("one", 4, False),
 )
 LAST_LAG = 12
-LATE = 2
+LATE_P2, LATE_P3 = 2, 3
 
 
 def dot(a, b, dims):
@@ -104,7 +106,7 @@
     (W, WX, POOL, A1, S1, A2, S2, N2, A3, S3, N3, U, GM, GH, XR, ST, TG, V640, V1280, VX, AC, VS) = rest[:22]
     (l_in, l_w, o_s, x_s, x_r, ha_s, ha_r, hg_s, hg_r) = rest[22:31]
     if fused:
-        (VF, VG, CR, KEEP, GIVE, YR, ZR, YX, VR, g_s, vg_r, ga_r, gc_r, wx_r, wc_r, r_s, rc_s, rc_r, ry_r, rz_r, yx_s, fy_r, fc_r, vr_s, vr_r) = rest[31:]
+        (VF, VG, CR, KEEP, GIVE, YR, ZR, YX, VR, g_s, gg_r, vg_r, ga_r, gc_r, wx_r, wc_r, r_s, rc_s, rc_r, ry_r, rz_r, yx_s, fy_r, fc_r, vr_s, vr_r) = rest[31:]
 
     sec = lax.axis_index("section")
     seq = lax.axis_index("seq")
@@ -170,7 +172,7 @@
     def piece(ref, b, s, half):
         return ref.at[b, pl.ds(pl.multiple_of(s * PART + half * HALF, 16), HALF), :]
 
-    UP, DOWN, Y_, CORE_, X_, XC_, V_ = range(7)
+    UP, DOWN, Y_, CORE_, X_, XC_, V_, G_ = range(8)
 
     def gz(b, s, to_up):
         spot = piece(W, b, s, core)
@@ -207,8 +209,21 @@
         s, d = others[i]
         return remote(VG.at[sec * SHARDS + ten], VG.at[sec * SHARDS + ten], g_s.at[V_], vg_r.at[0], (lax.rem(sec + s, 2), seq, lax.rem(ten + d, SHARDS)))
 
-    mine = lambda b: jnp.logical_or(b == BLOCKS - 1, lax.rem(b, 2) == y)
-    def send_own(b):
+    def gg(s):
+        return remote(piece(W, jnp.where(first, LAST, GUEST), s, core), piece(W, jnp.where(first, GUEST, LAST), s, core), g_s.at[G_], gg_r.at[s], at_x)
+
+    def turn(j):
+        return jnp.where(first, j, jnp.where(j < GUEST_TURN, j, jnp.where(j == GUEST_TURN, GUEST, j - 1)))
+
+    turns = jnp.where(first, BLOCKS, BLOCKS + 1)
+    mine = lambda b: jnp.where(b < LAST, lax.rem(b, 2) == y, jnp.logical_not(first))
+    def send_own(j):
+        b = turn(j)
+
+        @pl.when(b == GUEST)
+        def _():
+            gg(ten).wait_recv()
+
         @pl.when(jnp.logical_and(mine(b), ten < SHARDS - 1))
         def _():
             gz(b, ten, True).start()
@@ -222,22 +237,30 @@
             gx(b, ten).start()
 
     def gather_begin():
-        for b in range(LEAD):
-            own[b].wait()
-            send_own(b)
+        for j in range(2):
+            own[j].wait()
+            send_own(j)
+        for copy in own[2:]:
+            copy.wait()
+
+        @pl.when(first)
+        def _():
+            gg(ten).start()
+
         for i in range(len(others)):
             gv(i).start()
-        for copy in own[LEAD:]:
-            copy.wait()
+        for j in range(2, LEAD):
+            send_own(j)
 
     def gather_step(k):
-        @pl.when(k + LEAD < BLOCKS)
+        @pl.when(k + LEAD < turns)
         def _():
             send_own(k + LEAD)
 
         for d in range(1, SHARDS):
-            b = k - (d - 1)
-            ok = jnp.logical_and(b >= 0, b < BLOCKS)
+            j = k - (d - 1)
+            b = turn(j)
+            ok = jnp.logical_and(j >= 0, j < turns)
             for above in (False, True):
                 s = ten + d if above else ten - d
                 there = jnp.logical_and(ok, s < SHARDS if above else s >= 0)
@@ -251,35 +274,50 @@
                     def _():
                         gz(b, s, not above).start()
 
-                    @pl.when(b < BLOCKS - 1)
+                    @pl.when(b < LAST)
                     def _():
                         gy(b, s).start()
 
-                    gc(b, s).start()
+                    @pl.when(b < GUEST)
+                    def _():
+                        gc(b, s).start()
+
+                    @pl.when(b == GUEST)
+                    def _():
+                        gg(s).start()
 
                     @pl.when(wanted(b))
                     def _():
                         gx(b, s).start()
 
         for d in range(1, SHARDS):
-            b = k - d - Y_LAG
-            ok = jnp.logical_and(b >= 0, b < BLOCKS)
+            j = k - d - Y_LAG
+            b = turn(j)
+            ok = jnp.logical_and(j >= 0, j < turns)
             for above in (False, True):
                 s = ten + d if above else ten - d
                 there = jnp.logical_and(ok, s < SHARDS if above else s >= 0)
 
                 @pl.when(jnp.logical_and(there, jnp.logical_not(mine(b))))
                 def _():
-                    gy(b, s).wait_recv()
+                    @pl.when(b < LAST)
+                    def _():
+                        gy(b, s).wait_recv()
+
+                    @pl.when(b == LAST)
+                    def _():
+                        gg(s).wait_recv()
+
                     gc(b, s).start()
 
                     @pl.when(wanted(b))
                     def _():
                         gx(b, s).start()
 
-        b = k - C_LAG
-
-        @pl.when(jnp.logical_and(b >= 0, b < BLOCKS))
+        j = k - C_LAG
+        b = turn(j)
+
+        @pl.when(jnp.logical_and(jnp.logical_and(j >= 0, j < turns), b < GUEST))
         def _():
             gc_here(b)
 
@@ -299,14 +337,20 @@
         left(g_s.at[CORE_], BLOCKS * (SHARDS - 1) * HALF)
         left(g_s.at[X_], 2 * SHARDS * HALF)
         left(g_s.at[XC_], 2 * SHARDS * HALF)
-        for z in range(SHARDS):
-
-            @pl.when(ten == z)
-            def _():
-                if z < SHARDS - 1:
-                    left(g_s.at[UP], 5 * (z + 1) * HALF)
-                if z > 0:
-                    left(g_s.at[DOWN], 5 * (SHARDS - z) * HALF)
+        for who, count, pieces in ((0, 4, 1), (1, 6, SHARDS - 1)):
+
+            @pl.when(sec == who)
+            def _():
+                left(g_s.at[G_], pieces * HALF)
+
+            for z in range(SHARDS):
+
+                @pl.when(jnp.logical_and(sec == who, ten == z))
+                def _():
+                    if z < SHARDS - 1:
+                        left(g_s.at[UP], count * (z + 1) * HALF)
+                    if z > 0:
+                        left(g_s.at[DOWN], count * (SHARDS - z) * HALF)
 
     def vectors():
         lines = VG.at[pl.ds(0, len(others))]
@@ -395,9 +439,10 @@
         unroll(LEN // TILE, tile2)
         halo(A2, ha_s, ha_r, m, reach, True)
 
-    def stage_b(m, span, relay):
+    def stage_b(m, span):
         halo(A2, ha_s, ha_r, m, 2 * span, False)
-        TG[0:LEN, :] = sum(dot(A2[m, pl.ds(LEN + (t - 2) * span, LEN), :], W[4 + t], NT) for t in (2, 0, 1, 3, 4))
+        taps = [A2[m, pl.ds(LEN + (t - 2) * span, LEN), :] for t in range(5)]
+        TG[0:LEN, :] = dot(jnp.concatenate(taps, axis=1), jnp.concatenate([W[4 + t] for t in range(5)], axis=1), NT)
 
         def tile(i):
             r = i * TILE
@@ -413,8 +458,8 @@
             ST[at, 3:4] = inverse
 
         unroll(LEN // TILE, tile)
-        if relay:
-            x_send(m, A3).start()
+
+    def stage_out(m):
         here = rows(0, m)
         for h in range(2):
             mixed = dot(A3[here, :], W[2 + h], NN) + V1280[h, 0:1, :]
@@ -470,31 +515,34 @@
 
     def back_three(m):
         here = rows(0, m)
-        TG[LEN : 2 * LEN, :] = dot(U[0, here, :], W[2], NT) + dot(U[1, here, :], W[3], NT)
-
-    def stage_p1(m, reach):
-        back_three(m)
-
-        def tile(i):
-            r = i * TILE
-            at = rows(0, m, r, TILE)
-            y_ = TG[pl.ds(LEN + r, TILE), :] * S3[at, :].astype(f32)
-            normed = N3[at, :].astype(f32)
-            (grad,) = norm_back([y_], [normed], ST[at, 3:4], [V640[4:5, :]], H)
-            low = grad.astype(bf16)
-            GM[m, pl.ds(pl.multiple_of(LEN + r, 16), TILE), :] = low
-            AC[4] += eights(y_ * normed)
-            AC[5] += eights(y_)
-            AC[1] += eights(low.astype(f32))
-            for h in range(2):
-                AC[6 + h] += eights(U[h, at, :].astype(f32))
-
-        unroll(LEN // TILE, tile)
+        return dot(U[0, here, :], W[2], NT) + dot(U[1, here, :], W[3], NT)
+
+    def stage_back_three(m):
+        full_ = back_three(m)
+        high = full_.astype(bf16)
+        POOL[rows(SX_AT, m), :] = high
+        POOL[rows(SX_AT + ROWS, m), :] = (full_ - high.astype(f32)).astype(bf16)
+
+    def stage_p1(m, reach, kept_):
+        if kept_:
+            back = POOL[rows(SX_AT, m), :].astype(f32) + POOL[rows(SX_AT + ROWS, m), :].astype(f32)
+        else:
+            back = back_three(m)
+        at = rows(0, m)
+        y_ = back * S3[at, :].astype(f32)
+        normed = N3[at, :].astype(f32)
+        (grad,) = norm_back([y_], [normed], ST[at, 3:4], [V640[4:5, :]], H)
+        low = grad.astype(bf16)
+        GM[m, LEN : 2 * LEN, :] = low
         halo(GM, hg_s, hg_r, m, reach, True)
+        AC[4] += eights(y_ * normed)
+        AC[5] += eights(y_)
+        AC[1] += eights(low.astype(f32))
 
     def stage_p2(m, span, relay):
         halo(GM, hg_s, hg_r, m, 2 * span, False)
-        TG[0:LEN, :] = sum(dot(GM[m, pl.ds(LEN - (t - 2) * span, LEN), :], W[4 + t], NN) for t in (2, 0, 1, 3, 4))
+        taps = [GM[m, pl.ds(LEN - (t - 2) * span, LEN), :] for t in range(5)]
+        TG[0:LEN, :] = dot(jnp.concatenate(taps, axis=1), jnp.concatenate([W[4 + t] for t in range(5)]), NN)
 
         def tile(i):
             r = i * TILE
@@ -527,6 +575,7 @@
             grads = norm_back(ys, normeds, inverse, [V1280[h, 1:2, :] for h in range(2)], 2 * H)
             for h in range(2):
                 S1[h, at, :] = (U[h, at, :].astype(f32) + grads[h]).astype(bf16)
+                AC[6 + h] += eights(U[h, at, :].astype(f32))
                 AC[8 + h] += eights(ys[h] * normeds[h])
                 AC[10 + h] += eights(ys[h])
 
@@ -584,7 +633,7 @@
             def _():
                 stage_a(k - A_STEP, 2 * SPAN_0)
 
-        loop(BLOCKS + C_LAG, step)
+        loop(BLOCKS + 1 + C_LAG, step)
     else:
         for copy in own:
             copy.wait()
@@ -600,19 +649,28 @@
 
         if early == 0:
             loop(MICRO, firsts)
-        loop(MICRO, lambda m: stage_b(m, SPAN_0, True))
+
+        def leave(m):
+            stage_b(m, SPAN_0)
+            x_send(m, A3).start()
+            stage_out(m)
+
+        loop(MICRO, leave)
         if fused:
             others_blocks()
         loop(MICRO, stage_n)
 
         def backward(m):
             stage_q(m)
-            stage_p1(m, 2 * SPAN_0)
-
-            @pl.when(jnp.logical_and(m > 0, m < MICRO - 1))
-            def _():
-                stage_p2(m - 1, SPAN_0, False)
-                stage_p3(m - 1)
+            stage_p1(m, 2 * SPAN_0, False)
+
+            @pl.when(m < MICRO - LATE_P2)
+            def _():
+                stage_p2(m, SPAN_0, False)
+
+            @pl.when(m < MICRO - LATE_P3)
+            def _():
+                stage_p3(m)
 
         loop(MICRO, backward)
 
@@ -620,6 +678,7 @@
     def _():
         if fused:
             others_blocks()
+        loop(MICRO, stage_back_three)
 
         def both(k):
             @pl.when(k < MICRO)
@@ -630,12 +689,12 @@
 
             @pl.when(jnp.logical_and(k >= 1, k <= MICRO))
             def _():
-                stage_b(k - 1, SPAN_1, False)
-                stage_p1(k - 1, 2 * SPAN_1)
+                stage_b(k - 1, SPAN_1)
+                stage_p1(k - 1, 2 * SPAN_1, True)
 
             @pl.when(k == MICRO + 1)
             def _():
-                loop(MICRO - LATE, stage_p3)
+                loop(MICRO - LATE_P3, stage_p3)
 
             @pl.when(k >= 2)
             def _():
@@ -646,7 +705,7 @@
     def last_grad_hidden():
         @pl.when(first)
         def _():
-            loop(LATE, lambda m: stage_p2(m + MICRO - LATE, SPAN_0, False))
+            loop(LATE_P2, lambda m: stage_p2(m + MICRO - LATE_P2, SPAN_0, False))
 
     def small_gradients():
         for i in range(12):
@@ -673,11 +732,16 @@
         @pl.when(b >= 4)
         def _():
             at = pl.ds(pl.multiple_of(LEN + (b - 6) * span, 64), LEN)
-            TG[...] = sum(dot(GM[m, LEN : 2 * LEN, :], A2[m, at, :], TN) for m in range(MICRO))
+            TG[...] = dot(jnp.concatenate([GM[m, LEN : 2 * LEN, :] for m in range(MICRO)]), jnp.concatenate([A2[m, at, :] for m in range(MICRO)]), TN)
 
     if not fused:
         last_grad_hidden()
-        loop(LATE, lambda m: stage_p3(m + MICRO - LATE))
+        loop(LATE_P3, lambda m: stage_p3(m + MICRO - LATE_P3))
+
+        @pl.when(jnp.logical_not(first))
+        def _():
+            loop(MICRO, stage_out)
+
         small_gradients()
         relay_drain()
 
@@ -846,11 +910,15 @@
 
         late = t - BLOCKS
 
-        @pl.when(jnp.logical_and(late >= 0, late < LATE))
-        def _():
-            stage_p3(late + MICRO - LATE)
-
-        i = late - LATE
+        @pl.when(jnp.logical_and(late >= 0, late < LATE_P3))
+        def _():
+            stage_p3(late + MICRO - LATE_P3)
+
+        @pl.when(jnp.logical_and(jnp.logical_not(first), jnp.logical_and(late >= 0, late < MICRO)))
+        def _():
+            stage_out(late)
+
+        i = late - LATE_P3
 
         @pl.when(i == 0)
         def _():
@@ -887,7 +955,7 @@
     low = lambda *shape: pltpu.VMEM(shape, bf16)
     full = lambda *shape: pltpu.VMEM(shape, f32)
     scratch = [
-        low(BLOCKS, H, H),
+        low(BLOCKS + 1 if fused else BLOCKS, H, H),
         low(2, H, H),
         low(POOL_ROWS, H),
         low(2, ROWS, H),
@@ -930,9 +998,10 @@
             low(6, 4, HALF, H),
             low(3, HALF, H),
             full(4, 16, H),
-            dma(7),
+            dma(8),
+            dma(SHARDS),
             dma(1),
-            dma(BLOCKS, SHARDS),
+            dma(BLOCKS + 1, SHARDS),
             dma(BLOCKS),
             dma(2),
             dma(1),

time: 185 us -> 178 us (0.962)
  Pallas kernels: 184 us -> 177 us
    pallas_call x1, Pallas kernels: 178 us -> 170 us  [relay(): pl.pallas_call(functools.partial(relay_kernel, fused), out_shape=outs, in...]
where the time goes in v2:
time: 178 us
  Pallas kernels  177 us (99%)
    pallas_call x1, Pallas kernels, relay(): pl.pallas_call(functools.partial(relay_kernel, fused), out_shape=outs, in...  170 us
    pallas_call x1, Pallas kernels, unpacked(): pl.pallas_call(unpack_kernel, out_shape=[rows_like, rows_like, like(PART,...  6.78 us

profile of v2, /device:TPU:0, one launch (start us, length us, event | category | flops | bytes accessed | tf_op | source)
XLA Modules:
  0.0 177.9 jit_solution(8546493685357977244)
XLA Ops:
  0.7 170.2 %relay.1 = (bf16[4,256,1280]{2,1,0:T(8,128)(2,1)}, bf16[4,256,1280]{2,1,0:T(8,128)(2,1)}, bf16[9,160,640]{2,1,0:T(8,128)(2,1)}, f32[16,640]{1,0:T(8,128)}) custom-call(bf16[4,1,256,1280]{3,2,1,0:T(8,128)(2,1)} %refs_0_.1, bf16[4,1,256,1280]{3,2,1,0:T(8,128)(2,1)} %refs_1_.1, s32[4,1,256]{2,1,0:T(1,128)} %refs_2_.1, bf16[160,1280]{1,0:T(8,128)(2,1)} %bitcast.18, ...), custom_call_target="tpu_custom_call" | custom-call | flops 24999999488 | bytes 20000000 | tf_op jit(solution)/shard_map/relay/pallas_call | solution.py:1026
  170.9 6.8 %unpack.1 = (bf16[1,4,1,256,1280]{4,3,2,1,0:T(8,128)(2,1)}, bf16[1,4,1,256,1280]{4,3,2,1,0:T(8,128)(2,1)}, f32[160,1280]{1,0:T(8,128)}, f32[5,160,640]{2,1,0:T(8...) custom-call(bf16[4,256,1280]{2,1,0:T(8,128)(2,1)} %get-tuple-element, ...), custom_call_target="tpu_custom_call" | custom-call | tf_op jit(solution)/shard_map/unpack/pallas_call | solution.py:1075

commit v3 on v2

--- a/solution.py
+++ b/solution.py
@@ -31,6 +31,7 @@
 X_STEP = 9
 F_STEP = 2
 A_STEP = C_LAG + 1
+EARLY_A = 2
 LEAD = 3
 NN = (((1,), (0,)), ((), ()))
 NT = (((1,), (1,)), ((), ()))
@@ -629,7 +630,7 @@
             def _():
                 stage_first(k - F_STEP)
 
-            @pl.when(jnp.logical_and(first, jnp.logical_and(k >= A_STEP, k < A_STEP + MICRO)))
+            @pl.when(jnp.logical_and(first, jnp.logical_and(k >= A_STEP, k < A_STEP + EARLY_A)))
             def _():
                 stage_a(k - A_STEP, 2 * SPAN_0)
 
@@ -653,6 +654,12 @@
         def leave(m):
             stage_b(m, SPAN_0)
             x_send(m, A3).start()
+            if early:
+
+                @pl.when(m + EARLY_A < MICRO)
+                def _():
+                    stage_a(m + EARLY_A, 2 * SPAN_0)
+
             stage_out(m)
 
         loop(MICRO, leave)

time: 178 us -> 177 us (level)
  no operation moved by 1% of the time
where the time goes in v3:
time: 177 us; the launch traced here: 176 us
  Pallas kernels  176 us (99%)
    pallas_call x1, Pallas kernels, relay(): pl.pallas_call(functools.partial(relay_kernel, fused), out_shape=outs, in...  169 us
    pallas_call x1, Pallas kernels, unpacked(): pl.pallas_call(unpack_kernel, out_shape=[rows_like, rows_like, like(PART,...  6.78 us

profile of v3, /device:TPU:0, one launch (start us, length us, event | category | flops | bytes accessed | tf_op | source)
XLA Modules:
  0.0 176.4 jit_solution(11110766948196656360)
XLA Ops:
  0.7 168.8 %relay.1 = (bf16[4,256,1280]{2,1,0:T(8,128)(2,1)}, bf16[4,256,1280]{2,1,0:T(8,128)(2,1)}, bf16[9,160,640]{2,1,0:T(8,128)(2,1)}, f32[16,640]{1,0:T(8,128)}) custom-call(bf16[4,1,256,1280]{3,2,1,0:T(8,128)(2,1)} %refs_0_.1, bf16[4,1,256,1280]{3,2,1,0:T(8,128)(2,1)} %refs_1_.1, s32[4,1,256]{2,1,0:T(1,128)} %refs_2_.1, bf16[160,1280]{1,0:T(8,128)(2,1)} %bitcast.18, ...), custom_call_target="tpu_custom_call" | custom-call | flops 24999999488 | bytes 20000000 | tf_op jit(solution)/shard_map/relay/pallas_call | solution.py:1033
  169.4 6.8 %unpack.1 = (bf16[1,4,1,256,1280]{4,3,2,1,0:T(8,128)(2,1)}, bf16[1,4,1,256,1280]{4,3,2,1,0:T(8,128)(2,1)}, f32[160,1280]{1,0:T(8,128)}, f32[5,160,640]{2,1,0:T(8...) custom-call(bf16[4,256,1280]{2,1,0:T(8,128)(2,1)} %get-tuple-element, ...), custom_call_target="tpu_custom_call" | custom-call | tf_op jit(solution)/shard_map/unpack/pallas_call | solution.py:1082
